TPU v7x, 32 devices: a whole 2x2x4 slice. The times are simulated.
32 devices in a mesh: ens: 4 (over y, x), tile: 8 (over z, core).
Axes of the slice: x: 2, y: 2, z: 4, core: 2. Of those that a mesh axis runs over, the one named last changes fastest.
Arguments:
- surface: float32 [8192, 1024], P(('ens', 'tile')), parts along dimension 0, may hold values from -6 to 6
- flux_x: float32 [8192, 1024], P(('ens', 'tile')), parts along dimension 0, may hold values from -3 to 3
- flux_y: float32 [8192, 1024], P(('ens', 'tile')), parts along dimension 0, may hold values from -3 to 3
- celerity: float32 [8192, 1024], P(('ens', 'tile')), parts along dimension 0, may hold values from 0.05 to 0.45
- bed_depth: float32 [8192, 1024], P(('ens', 'tile')), parts along dimension 0, may hold values from 0.2 to 3
- roughness: float32 [8192, 1024], P(('ens', 'tile')), parts along dimension 0, may hold values from 0.2 to 2
- smoother: bfloat16 [256, 256], replicated, may hold values from -0.5 to 1.5
- block_plan: int32 [32, 4], P(('ens', 'tile')), parts along dimension 0, may hold values from 0 to 3, as said below
Outputs:
- new_surface: float32 [8192, 1024], P(('ens', 'tile')), parts along dimension 0
- new_flux_x: float32 [8192, 1024], P(('ens', 'tile')), parts along dimension 0
- new_flux_y: float32 [8192, 1024], P(('ens', 'tile')), parts along dimension 0
- resident: float32 [96, 2, 256, 256], P(('ens', 'tile')), parts along dimension 0
- energy: float32 [8], P('ens'), parts along dimension 0
There are 4 independent parts, one for each index of `ens`. A program takes and returns all parts, laid end to end along the dimension named above; an argument that names none is the same for every part. Nothing has to cross between parts.
Inputs may be any that keep to these rules, and one draw needn't show every extreme that they name: `block_plan`: codes per block: 0 dry, 1 to 3 wet with the slots of the steps. Every tile holds exactly one block of each code 1, 2 and 3 and one dry block, so every slot holds exactly one block.
All inputs are finite; a program needn't handle non-finite values.
Results may differ from a plain program's by a relative error of at most 0.022.
Values may be sent and summed in bfloat16 or wider, within the bound.
A program may use at most 64 MiB of HBM per device.

v0:
```python
import jax
import jax.numpy as jnp
from jax import lax
from jax.sharding import PartitionSpec as P

STEPS = 2
SUB = 12


def passed_along(value, axis, steps):
    count = lax.axis_size(axis)
    leading, last = (max(0, -steps), min(count, count - steps))
    return lax.ppermute(value, axis, [(source, source + steps) for source in range(leading, last)])


def from_behind(block, axis, distance):
    devices = range(lax.axis_size(axis))
    route = [((i - distance) % len(devices), i) for i in devices]
    return lax.ppermute(block, axis, route)


def soften(packed, drag_ratio, smoother):
    weight = drag_ratio.astype(jnp.float32)[:, None]
    settled = jnp.zeros(packed.shape, jnp.float32)
    for _ in range(SUB):
        partial_rows = jnp.einsum(
            "sfij,kj->sfik", packed, smoother, preferred_element_type=jnp.float32
        ).astype(jnp.bfloat16)
        mixed_full = jnp.einsum(
            "ki,sfij->sfkj", smoother, partial_rows, preferred_element_type=jnp.float32
        )
        settled = mixed_full / (1.0 + weight * jnp.abs(mixed_full))
        packed = settled.astype(jnp.bfloat16)
    return settled


def choose(stacked, plan_codes, wanted):
    view_shape = (plan_codes.shape[0],) + (1,) * (stacked.ndim - 1)
    picked = jnp.where(
        (plan_codes == wanted).reshape(view_shape), stacked, jnp.zeros((), stacked.dtype)
    )
    return jnp.sum(picked, axis=0)


def on_device(surface, flux_x, flux_y, celerity, bed_depth, roughness, smoother, block_plan):
    row_count, col_count = surface.shape
    half_cols = col_count // 2
    block_side = smoother.shape[0]
    block_count = col_count // block_side
    tile_count = lax.axis_size("tile")
    position = lax.axis_index("tile")
    top_edge = position == 0
    bottom_edge = position == tile_count - 1
    col_ids = jnp.arange(col_count, dtype=jnp.int32)
    right_edge = (col_ids % half_cols == half_cols - 1)[None, :]
    left_edge = (col_ids % half_cols == 0)[None, :]
    plan_codes = block_plan[0]
    code_view = plan_codes.reshape(block_count, 1, 1, 1)
    level, flow_x, flow_y = (surface, flux_x, flux_y)
    resident = jnp.zeros((3, 2, block_side, block_side), jnp.float32)
    for repeat in range(STEPS):
        below_row = passed_along(level[0:1], "tile", -1)
        below_row = jnp.where(bottom_edge, 0.0, below_row)
        ahead_rows = jnp.concatenate([level[1:], below_row], 0)
        flow_x = flow_x - celerity * (ahead_rows - level)
        right_cells = jnp.where(right_edge, 0.0, jnp.roll(level, -1, axis=1))
        flow_y = flow_y - celerity * (right_cells - level)
        above_row = passed_along(flow_x[row_count - 1 :], "tile", 1)
        above_row = jnp.where(top_edge, 0.0, above_row)
        behind_x = jnp.concatenate([above_row, flow_x[:-1]], 0)
        behind_y = jnp.where(left_edge, 0.0, jnp.roll(flow_y, 1, axis=1))
        level = level - (flow_x - behind_x) - (flow_y - behind_y)
        drag_ratio = (roughness / jnp.maximum(level + bed_depth, 1.0)).astype(jnp.bfloat16)
        fluxes = jnp.stack([flow_x, flow_y], 0)
        flux_blocks = jnp.stack(
            [
                fluxes[:, :, column_index * block_side : (column_index + 1) * block_side]
                for column_index in range(block_count)
            ],
            0,
        )
        drag_blocks = jnp.stack(
            [
                drag_ratio[:, column_index * block_side : (column_index + 1) * block_side]
                for column_index in range(block_count)
            ],
            0,
        )
        payload = jnp.concatenate([flux_blocks.astype(jnp.bfloat16), drag_blocks[:, None]], 1)
        own_first = choose(payload, plan_codes, 1)
        go_near = choose(payload, plan_codes, 2)
        go_far = choose(payload, plan_codes, 3)
        got_near = from_behind(go_near, "tile", 1)
        got_far = from_behind(go_far, "tile", 2)
        slots = jnp.stack([own_first, got_near, got_far], 0)
        results = soften(slots[:, :2], slots[:, 2], smoother)
        home_near = from_behind(results[1], "tile", -1)
        home_far = from_behind(results[2], "tile", -2)
        new_blocks = jnp.where(
            code_view == 1,
            results[0],
            jnp.where(code_view == 2, home_near, jnp.where(code_view == 3, home_far, flux_blocks)),
        )
        resident = results
        flow_x = jnp.concatenate(
            [new_blocks[column_index, 0] for column_index in range(block_count)], 1
        )
        flow_y = jnp.concatenate(
            [new_blocks[column_index, 1] for column_index in range(block_count)], 1
        )
    total_rows = tile_count * row_count
    row_index = position * row_count + jnp.arange(row_count, dtype=jnp.int32)
    row_weight = 1.0 + 2.0 * row_index.astype(jnp.float32) / total_rows
    squares = (row_weight[:, None] * level * level).reshape(row_count, 2, half_cols)
    term_pair = jnp.sum(squares, axis=(0, 2)) / (total_rows * half_cols)
    energy = lax.psum(term_pair, "tile")
    return (level, flow_x, flow_y, resident, energy)


def solution(mesh):
    in_specs = (
        P(("ens", "tile"), None),
        P(("ens", "tile"), None),
        P(("ens", "tile"), None),
        P(("ens", "tile"), None),
        P(("ens", "tile"), None),
        P(("ens", "tile"), None),
        P(),
        P(("ens", "tile"), None),
    )
    out_specs = (
        P(("ens", "tile"), None),
        P(("ens", "tile"), None),
        P(("ens", "tile"), None),
        P(("ens", "tile"), None, None, None),
        P("ens"),
    )
    return jax.shard_map(
        on_device, mesh=mesh, in_specs=in_specs, out_specs=out_specs, check_vma=False
    )
```

profile of v0, /device:TPU:0, one launch (start us, length us, event | category | flops | bytes accessed | tf_op | source)
XLA Modules:
  0.0 195.3 jit_solution(13021126170676835774)
XLA Ops:
  8.3 4.0 %collective-permute-start.1 = (f32[1,1024]{1,0:T(1,128)S(1)}, f32[1,1024]{1,0:T(1,128)S(1)}, u32[]{:S(2)}, u32[]{:S(2)}) collective-permute-start(f32[1,1024]{1,0:T(1,128)S(1)} %slice.236), channel_id=1, source_target_pairs={{0,1},{1,2},{2,3},{3,4},{4,5},{5,6},{6,7},{8,9},{9,10},{10,11},{11... | collective-permute-start | bytes 12296 | tf_op jit(solution)/shard_map/ppermute | solution.py:13
  20.2 7.7 %collective-permute-done.2 = bf16[3,256,256]{2,1,0:T(8,128)(2,1)S(1)} collective-permute-done((bf16[3,256,256]{2,1,0:T(8,128)(2,1)S(1)}, bf16[3,256,256]{2,1,0:T(8,128)(2,1)S(1)}, u32[]{:S(2)}, u32[]{:S(2)}) %collective-permute-start.2) | collective-permute-done | bytes 393248 | tf_op jit(solution)/shard_map/ppermute | solution.py:19
  27.9 4.6 %collective-permute-done.3 = bf16[3,256,256]{2,1,0:T(8,128)(2,1)S(1)} collective-permute-done((bf16[3,256,256]{2,1,0:T(8,128)(2,1)S(1)}, bf16[3,256,256]{2,1,0:T(8,128)(2,1)S(1)}, u32[]{:S(2)}, u32[]{:S(2)}) %collective-permute-start.3) | collective-permute-done | bytes 393248 | tf_op jit(solution)/shard_map/ppermute | solution.py:19
  34.4 3.1 %fusion.48 = bf16[3,2,256,256]{2,3,1,0:T(8,128)(2,1)} fusion(bf16[1,3,256,256]{3,2,1,0:T(8,128)(2,1)} %bitcast.486, bf16[1,3,256,256]{3,2,1,0:T(8,128)(2,1)} %bitcast.482, bf16[1,3,256,256]{3,2,1,0:T(8,128)(2,1)} %bitcast.478, f32[3,256,256]{1,2,0:T(8,128)} %copy.32, bf16[256,256]{1,0:T(8,128)(2,1)S(1)} %copy-done), kind=kOutput, calls=%fused_computation.121 | convolution fusion | flops 408551424 | bytes 2883584 | tf_op jit(solution)/shard_map/ki,sfij->sfkj/dot_general | solution.py:29
  37.6 2.9 %fusion.49 = bf16[3,2,256,256]{2,3,1,0:T(8,128)(2,1)} fusion(bf16[3,2,256,256]{2,3,1,0:T(8,128)(2,1)} %fusion.48, f32[3,256,256]{1,2,0:T(8,128)S(1)} %copy-done.17, bf16[256,256]{1,0:T(8,128)(2,1)S(1)} %copy-done), kind=kOutput, calls=%fused_computation.122 | convolution fusion | flops 405012480 | bytes 2490368 | tf_op jit(solution)/shard_map/ki,sfij->sfkj/dot_general | solution.py:29
  40.5 2.9 %fusion.50 = bf16[3,2,256,256]{2,3,1,0:T(8,128)(2,1)} fusion(bf16[3,2,256,256]{2,3,1,0:T(8,128)(2,1)} %fusion.49, f32[3,256,256]{1,2,0:T(8,128)S(1)} %copy-done.17, bf16[256,256]{1,0:T(8,128)(2,1)S(1)} %copy-done), kind=kOutput, calls=%fused_computation.123 | convolution fusion | flops 405012480 | bytes 2490368 | tf_op jit(solution)/shard_map/ki,sfij->sfkj/dot_general | solution.py:29
  43.4 2.9 %fusion.51 = bf16[3,2,256,256]{2,3,1,0:T(8,128)(2,1)} fusion(bf16[3,2,256,256]{2,3,1,0:T(8,128)(2,1)} %fusion.50, f32[3,256,256]{1,2,0:T(8,128)S(1)} %copy-done.17, bf16[256,256]{1,0:T(8,128)(2,1)S(1)} %copy-done), kind=kOutput, calls=%fused_computation.124 | convolution fusion | flops 405012480 | bytes 2490368 | tf_op jit(solution)/shard_map/ki,sfij->sfkj/dot_general | solution.py:29
  46.3 2.9 %fusion.52 = bf16[3,2,256,256]{2,3,1,0:T(8,128)(2,1)} fusion(bf16[3,2,256,256]{2,3,1,0:T(8,128)(2,1)} %fusion.51, f32[3,256,256]{1,2,0:T(8,128)S(1)} %copy-done.17, bf16[256,256]{1,0:T(8,128)(2,1)S(1)} %copy-done), kind=kOutput, calls=%fused_computation.125 | convolution fusion | flops 405012480 | bytes 2490368 | tf_op jit(solution)/shard_map/ki,sfij->sfkj/dot_general | solution.py:29
  49.2 2.9 %fusion.53 = bf16[3,2,256,256]{2,3,1,0:T(8,128)(2,1)} fusion(bf16[3,2,256,256]{2,3,1,0:T(8,128)(2,1)} %fusion.52, f32[3,256,256]{1,2,0:T(8,128)S(1)} %copy-done.17, bf16[256,256]{1,0:T(8,128)(2,1)S(1)} %copy-done), kind=kOutput, calls=%fused_computation.126 | convolution fusion | flops 405012480 | bytes 2490368 | tf_op jit(solution)/shard_map/ki,sfij->sfkj/dot_general | solution.py:29
  52.1 2.9 %fusion.54 = bf16[3,2,256,256]{2,3,1,0:T(8,128)(2,1)} fusion(bf16[3,2,256,256]{2,3,1,0:T(8,128)(2,1)} %fusion.53, f32[3,256,256]{1,2,0:T(8,128)S(1)} %copy-done.17, bf16[256,256]{1,0:T(8,128)(2,1)S(1)} %copy-done), kind=kOutput, calls=%fused_computation.127 | convolution fusion | flops 405012480 | bytes 2490368 | tf_op jit(solution)/shard_map/ki,sfij->sfkj/dot_general | solution.py:29
  55.0 2.9 %fusion.55 = bf16[3,2,256,256]{2,3,1,0:T(8,128)(2,1)} fusion(bf16[3,2,256,256]{2,3,1,0:T(8,128)(2,1)} %fusion.54, f32[3,256,256]{1,2,0:T(8,128)S(1)} %copy-done.17, bf16[256,256]{1,0:T(8,128)(2,1)S(1)} %copy-done), kind=kOutput, calls=%fused_computation.128 | convolution fusion | flops 405012480 | bytes 2490368 | tf_op jit(solution)/shard_map/ki,sfij->sfkj/dot_general | solution.py:29
  57.9 2.9 %fusion.56 = bf16[3,2,256,256]{2,3,1,0:T(8,128)(2,1)} fusion(bf16[3,2,256,256]{2,3,1,0:T(8,128)(2,1)} %fusion.55, f32[3,256,256]{1,2,0:T(8,128)S(1)} %copy-done.17, bf16[256,256]{1,0:T(8,128)(2,1)S(1)} %copy-done), kind=kOutput, calls=%fused_computation.129 | convolution fusion | flops 405012480 | bytes 2490368 | tf_op jit(solution)/shard_map/ki,sfij->sfkj/dot_general | solution.py:29
  60.8 2.9 %fusion.57 = bf16[3,2,256,256]{2,3,1,0:T(8,128)(2,1)} fusion(bf16[3,2,256,256]{2,3,1,0:T(8,128)(2,1)} %fusion.56, f32[3,256,256]{1,2,0:T(8,128)S(1)} %copy-done.17, bf16[256,256]{1,0:T(8,128)(2,1)S(1)} %copy-done), kind=kOutput, calls=%fused_computation.130 | convolution fusion | flops 405012480 | bytes 2490368 | tf_op jit(solution)/shard_map/ki,sfij->sfkj/dot_general | solution.py:29
  63.7 2.9 %fusion.58 = bf16[3,2,256,256]{2,3,1,0:T(8,128)(2,1)} fusion(bf16[3,2,256,256]{2,3,1,0:T(8,128)(2,1)} %fusion.57, f32[3,256,256]{1,2,0:T(8,128)S(1)} %copy-done.17, bf16[256,256]{1,0:T(8,128)(2,1)S(1)} %copy-done), kind=kOutput, calls=%fused_computation.131 | convolution fusion | flops 405012480 | bytes 2490368 | tf_op jit(solution)/shard_map/ki,sfij->sfkj/dot_general | solution.py:29
  66.6 3.2 %bitcast_divide_fusion.12 = f32[3,2,256,256]{2,3,1,0:T(8,128)} fusion(bf16[3,2,256,256]{2,3,1,0:T(8,128)(2,1)} %fusion.58, f32[3,256,256]{1,2,0:T(8,128)S(1)} %copy-done.17, bf16[256,256]{1,0:T(8,128)(2,1)S(1)} %copy-done), kind=kOutput, calls=%fused_computation.66 | convolution fusion | flops 404619264 | bytes 3276800 | tf_op jit(solution)/shard_map/ki,sfij->sfkj/dot_general | solution.py:29
  69.7 2.6 %slice_bitcast_fusion.5 = (f32[2,256,256]{1,2,0:T(8,128)}, f32[2,256,256]{1,2,0:T(8,128)}, f32[2,256,256]{1,2,0:T(8,128)}) fusion(f32[3,2,256,256]{2,3,1,0:T(8,128)} %bitcast_divide_fusion.12), kind=kLoop, calls=%fused_computation.227 | loop fusion | bytes 3145728 | tf_op jit(solution)/shard_map/squeeze | solution.py:101
  72.3 4.0 %collective-permute-start.4 = (f32[2,256,256]{1,2,0:T(8,128)}, f32[2,256,256]{1,2,0:T(8,128)}, u32[]{:S(2)}, u32[]{:S(2)}) collective-permute-start(f32[2,256,256]{1,2,0:T(8,128)} %get-tuple-element.63), channel_id=1, source_target_pairs={{1,0},{2,1},{3,2},{4,3},{5,4},{6,5},{7,6},{0,7},{9,8},{10,9},{11,1... | collective-permute-start | bytes 1572872 | tf_op jit(solution)/shard_map/ppermute | solution.py:19
  82.9 5.5 %collective-permute-done.4 = f32[2,256,256]{1,2,0:T(8,128)} collective-permute-done((f32[2,256,256]{1,2,0:T(8,128)}, f32[2,256,256]{1,2,0:T(8,128)}, u32[]{:S(2)}, u32[]{:S(2)}) %collective-permute-start.4) | collective-permute-done | bytes 524320 | tf_op jit(solution)/shard_map/ppermute | solution.py:19
  90.4 3.6 %collective-permute-done.5 = f32[2,256,256]{1,2,0:T(8,128)} collective-permute-done((f32[2,256,256]{1,2,0:T(8,128)}, f32[2,256,256]{1,2,0:T(8,128)}, u32[]{:S(2)}, u32[]{:S(2)}) %collective-permute-start.5) | collective-permute-done | bytes 524320 | tf_op jit(solution)/shard_map/ppermute | solution.py:19
  100.3 6.0 %collective-permute-start.7 = (f32[1,1024]{1,0:T(1,128)S(1)}, f32[1,1024]{1,0:T(1,128)S(1)}, u32[]{:S(2)}, u32[]{:S(2)}) collective-permute-start(f32[1,1024]{1,0:T(1,128)S(1)} %slice.259), channel_id=1, source_target_pairs={{0,1},{1,2},{2,3},{3,4},{4,5},{5,6},{6,7},{8,9},{9,10},{10,11},{11... | collective-permute-start | bytes 12296 | tf_op jit(solution)/shard_map/ppermute | solution.py:13
  112.8 10.8 %collective-permute-done.8 = bf16[3,256,256]{2,1,0:T(8,128)(2,1)S(1)} collective-permute-done((bf16[3,256,256]{2,1,0:T(8,128)(2,1)S(1)}, bf16[3,256,256]{2,1,0:T(8,128)(2,1)S(1)}, u32[]{:S(2)}, u32[]{:S(2)}) %collective-permute-start.8) | collective-permute-done | bytes 393248 | tf_op jit(solution)/shard_map/ppermute | solution.py:19
  126.7 3.0 %fusion.59 = bf16[3,2,256,256]{2,3,1,0:T(8,128)(2,1)} fusion(bf16[1,3,256,256]{3,2,1,0:T(8,128)(2,1)} %bitcast.488, bf16[1,3,256,256]{3,2,1,0:T(8,128)(2,1)S(1)} %bitcast.484, bf16[1,3,256,256]{3,2,1,0:T(8,128)(2,1)S(1)} %bitcast.480, f32[3,256,256]{1,2,0:T(8,128)} %copy.60, bf16[256,256]{1,0:T(8,128)(2,1)S(1)} %copy-done), kind=kOutput, calls=%fused_computation.132 | convolution fusion | flops 408551424 | bytes 2883584 | tf_op jit(solution)/shard_map/ki,sfij->sfkj/dot_general | solution.py:29
  152.1 4.1 %collective-permute-start.10 = (f32[2,256,256]{1,2,0:T(8,128)}, f32[2,256,256]{1,2,0:T(8,128)}, u32[]{:S(2)}, u32[]{:S(2)}) collective-permute-start(f32[2,256,256]{1,2,0:T(8,128)} %get-tuple-element.60), channel_id=1, source_target_pairs={{1,0},{2,1},{3,2},{4,3},{5,4},{6,5},{7,6},{0,7},{9,8},{10,9},{11,1... | collective-permute-start | bytes 1572872 | tf_op jit(solution)/shard_map/ppermute | solution.py:19
  156.9 29.1 %psum.7 = f32[2]{0:T(128)} all-reduce(f32[2]{0:T(128)S(1)} %broadcast_multiply_fusion), channel_id=1, replica_groups=mesh['ens'=4,'tile'=8] {'tile'}, use_global_device_ids=true, to_apply=%region_8.9 | all-reduce | flops 2 | bytes 16 | tf_op jit(solution)/shard_map/psum | solution.py:116
  (126 shorter events, 73.8 us)
Async XLA Ops:
  0.6 33.8 %copy-start = (bf16[256,256]{1,0:T(8,128)(2,1)S(1)}, bf16[256,256]{1,0:T(8,128)(2,1)}, u32[]{:S(2)}) copy-start(bf16[256,256]{1,0:T(8,128)(2,1)} %param.14) | copy-start | bytes 393220
  0.6 4.2 %copy-start.1 = (f32[256,1024]{1,0:T(8,128)S(1)}, f32[256,1024]{1,0:T(8,128)}, u32[]{:S(2)}) copy-start(f32[256,1024]{1,0:T(8,128)} %param.8) | copy-start | bytes 3145732
  1.5 3.7 %collective-permute-start = (f32[1,1024]{1,0:T(1,128)S(1)}, f32[1,1024]{1,0:T(1,128)S(1)}, u32[]{:S(2)}, u32[]{:S(2)}) collective-permute-start(f32[1,1024]{1,0:T(1,128)S(1)} %slice.179), channel_id=1, source_target_pairs={{1,0},{2,1},{3,2},{4,3},{5,4},{6,5},{7,6},{9,8},{10,9},{11,10},{12... | collective-permute-start | bytes 12296 | tf_op jit(solution)/shard_map/ppermute | solution.py:13
  8.3 5.3 %collective-permute-start.1 = (f32[1,1024]{1,0:T(1,128)S(1)}, f32[1,1024]{1,0:T(1,128)S(1)}, u32[]{:S(2)}, u32[]{:S(2)}) collective-permute-start(f32[1,1024]{1,0:T(1,128)S(1)} %slice.236), channel_id=1, source_target_pairs={{0,1},{1,2},{2,3},{3,4},{4,5},{5,6},{6,7},{8,9},{9,10},{10,11},{11... | collective-permute-start | bytes 12296 | tf_op jit(solution)/shard_map/ppermute | solution.py:13
  12.6 1.6 copy-start.8
  12.6 1.9 copy-start.10
  16.9 15.6 %copy-start.16 = (bf16[3,256,256]{2,1,0:T(8,128)(2,1)}, bf16[3,256,256]{2,1,0:T(8,128)(2,1)S(1)}, u32[]{:S(2)}) copy-start(bf16[3,256,256]{2,1,0:T(8,128)(2,1)S(1)} %get-tuple-element.23) | copy-start | bytes 1179652
  16.9 11.0 %collective-permute-start.2 = (bf16[3,256,256]{2,1,0:T(8,128)(2,1)S(1)}, bf16[3,256,256]{2,1,0:T(8,128)(2,1)S(1)}, u32[]{:S(2)}, u32[]{:S(2)}) collective-permute-start(bf16[3,256,256]{2,1,0:T(8,128)(2,1)S(1)} %get-tuple-element.24), channel_id=1, source_target_pairs={{7,0},{0,1},{1,2},{2,3},{3,4},{4,5},{5,6},{6,7},{15,8},{8,9},{9,10... | collective-permute-start | bytes 1179656 | tf_op jit(solution)/shard_map/ppermute | solution.py:19
  18.6 13.9 %collective-permute-start.3 = (bf16[3,256,256]{2,1,0:T(8,128)(2,1)S(1)}, bf16[3,256,256]{2,1,0:T(8,128)(2,1)S(1)}, u32[]{:S(2)}, u32[]{:S(2)}) collective-permute-start(bf16[3,256,256]{2,1,0:T(8,128)(2,1)S(1)} %get-tuple-element.25), channel_id=1, source_target_pairs={{6,0},{7,1},{0,2},{1,3},{2,4},{3,5},{4,6},{5,7},{14,8},{15,9},{8,1... | collective-permute-start | bytes 1179656 | tf_op jit(solution)/shard_map/ppermute | solution.py:19
  27.9 4.6 %copy-start.19 = (bf16[3,256,256]{2,1,0:T(8,128)(2,1)}, bf16[3,256,256]{2,1,0:T(8,128)(2,1)S(1)}, u32[]{:S(2)}) copy-start(bf16[3,256,256]{2,1,0:T(8,128)(2,1)S(1)} %collective-permute-done.2) | copy-start | bytes 1179652
  34.4 3.1 %copy-start.17 = (f32[3,256,256]{1,2,0:T(8,128)S(1)}, f32[3,256,256]{1,2,0:T(8,128)}, u32[]{:S(2)}) copy-start(f32[3,256,256]{1,2,0:T(8,128)} %copy.32) | copy-start | bytes 2359300
  72.3 16.1 %collective-permute-start.4 = (f32[2,256,256]{1,2,0:T(8,128)}, f32[2,256,256]{1,2,0:T(8,128)}, u32[]{:S(2)}, u32[]{:S(2)}) collective-permute-start(f32[2,256,256]{1,2,0:T(8,128)} %get-tuple-element.63), channel_id=1, source_target_pairs={{1,0},{2,1},{3,2},{4,3},{5,4},{6,5},{7,6},{0,7},{9,8},{10,9},{11,1... | collective-permute-start | bytes 1572872 | tf_op jit(solution)/shard_map/ppermute | solution.py:19
  76.3 17.7 %collective-permute-start.5 = (f32[2,256,256]{1,2,0:T(8,128)}, f32[2,256,256]{1,2,0:T(8,128)}, u32[]{:S(2)}, u32[]{:S(2)}) collective-permute-start(f32[2,256,256]{1,2,0:T(8,128)} %get-tuple-element.62), channel_id=1, source_target_pairs={{2,0},{3,1},{4,2},{5,3},{6,4},{7,5},{0,6},{1,7},{10,8},{11,9},{12,... | collective-permute-start | bytes 1572872 | tf_op jit(solution)/shard_map/ppermute | solution.py:19
  76.8 3.9 %collective-permute-start.6 = (f32[1,1024]{1,0:T(1,128)S(1)}, f32[1,1024]{1,0:T(1,128)S(1)}, u32[]{:S(2)}, u32[]{:S(2)}) collective-permute-start(f32[1,1024]{1,0:T(1,128)S(1)} %slice.258), channel_id=1, source_target_pairs={{1,0},{2,1},{3,2},{4,3},{5,4},{6,5},{7,6},{9,8},{10,9},{11,10},{12... | collective-permute-start | bytes 12296 | tf_op jit(solution)/shard_map/ppermute | solution.py:13
  80.7 15.3 %copy-start.3 = (f32[1,2,256,256]{3,2,1,0:T(8,128)S(1)}, f32[1,2,256,256]{3,2,1,0:T(8,128)}, u32[]{:S(2)}) copy-start(f32[1,2,256,256]{3,2,1,0:T(8,128)} %copy-done.2) | copy-start | bytes 1572868
  80.7 15.3 %copy-start.5 = (f32[1,2,256,256]{3,2,1,0:T(8,128)S(1)}, f32[1,2,256,256]{3,2,1,0:T(8,128)}, u32[]{:S(2)}) copy-start(f32[1,2,256,256]{3,2,1,0:T(8,128)} %copy-done.4) | copy-start | bytes 1572868
  97.8 1.8 copy-start.15
  100.3 7.1 %collective-permute-start.7 = (f32[1,1024]{1,0:T(1,128)S(1)}, f32[1,1024]{1,0:T(1,128)S(1)}, u32[]{:S(2)}, u32[]{:S(2)}) collective-permute-start(f32[1,1024]{1,0:T(1,128)S(1)} %slice.259), channel_id=1, source_target_pairs={{0,1},{1,2},{2,3},{3,4},{4,5},{5,6},{6,7},{8,9},{9,10},{10,11},{11... | collective-permute-start | bytes 12296 | tf_op jit(solution)/shard_map/ppermute | solution.py:13
  110.9 12.7 %collective-permute-start.8 = (bf16[3,256,256]{2,1,0:T(8,128)(2,1)S(1)}, bf16[3,256,256]{2,1,0:T(8,128)(2,1)S(1)}, u32[]{:S(2)}, u32[]{:S(2)}) collective-permute-start(bf16[3,256,256]{2,1,0:T(8,128)(2,1)S(1)} %get-tuple-element.21), channel_id=1, source_target_pairs={{7,0},{0,1},{1,2},{2,3},{3,4},{4,5},{5,6},{6,7},{15,8},{8,9},{9,10... | collective-permute-start | bytes 1179656 | tf_op jit(solution)/shard_map/ppermute | solution.py:19
  111.0 13.8 %collective-permute-start.9 = (bf16[3,256,256]{2,1,0:T(8,128)(2,1)S(1)}, bf16[3,256,256]{2,1,0:T(8,128)(2,1)S(1)}, u32[]{:S(2)}, u32[]{:S(2)}) collective-permute-start(bf16[3,256,256]{2,1,0:T(8,128)(2,1)S(1)} %get-tuple-element.22), channel_id=1, source_target_pairs={{6,0},{7,1},{0,2},{1,3},{2,4},{3,5},{4,6},{5,7},{14,8},{15,9},{8,1... | collective-permute-start | bytes 1179656 | tf_op jit(solution)/shard_map/ppermute | solution.py:19
  126.7 3.0 %copy-start.18 = (f32[3,256,256]{1,2,0:T(8,128)S(1)}, f32[3,256,256]{1,2,0:T(8,128)}, u32[]{:S(2)}) copy-start(f32[3,256,256]{1,2,0:T(8,128)} %copy.60) | copy-start | bytes 2359300
  152.1 36.8 %collective-permute-start.10 = (f32[2,256,256]{1,2,0:T(8,128)}, f32[2,256,256]{1,2,0:T(8,128)}, u32[]{:S(2)}, u32[]{:S(2)}) collective-permute-start(f32[2,256,256]{1,2,0:T(8,128)} %get-tuple-element.60), channel_id=1, source_target_pairs={{1,0},{2,1},{3,2},{4,3},{5,4},{6,5},{7,6},{0,7},{9,8},{10,9},{11,1... | collective-permute-start | bytes 1572872 | tf_op jit(solution)/shard_map/ppermute | solution.py:19
  156.3 33.9 %collective-permute-start.11 = (f32[2,256,256]{1,2,0:T(8,128)}, f32[2,256,256]{1,2,0:T(8,128)}, u32[]{:S(2)}, u32[]{:S(2)}) collective-permute-start(f32[2,256,256]{1,2,0:T(8,128)} %get-tuple-element.59), channel_id=1, source_target_pairs={{2,0},{3,1},{4,2},{5,3},{6,4},{7,5},{0,6},{1,7},{10,8},{11,9},{12,... | collective-permute-start | bytes 1572872 | tf_op jit(solution)/shard_map/ppermute | solution.py:19
  187.6 4.6 %copy-start.7 = (f32[1,2,256,256]{3,2,1,0:T(8,128)S(1)}, f32[1,2,256,256]{3,2,1,0:T(8,128)}, u32[]{:S(2)}) copy-start(f32[1,2,256,256]{3,2,1,0:T(8,128)} %copy-done.6) | copy-start | bytes 1572868
  (11 other events, 11.6 us)
where the time goes:
time: 197 us; the launch traced here: 195 us
  matrix products  59.5 us (30%)
  waiting for transfers between devices  33.3 us (17%)
  local copies, waits for them, and re-layouts  30.5 us (15%)
  blocking collectives  29.1 us (15%)
  starting transfers between devices  27.1 us (14%)
  other arithmetic  14.6 us (7%)
    dot_general x24, matrix products, soften(): jnp.einsum('ki,sfij->sfkj', smoother, partial_rows, preferred_element_typ...  59.5 us
    ppermute x8, waiting for transfers between devices, from_behind(): return lax.ppermute(block, axis, route)  33.3 us
    psum x1, blocking collectives, on_device(): energy = lax.psum(term_pair, 'tile')  29.1 us
    ppermute x8, starting transfers between devices, from_behind(): return lax.ppermute(block, axis, route)  14.2 us
    ppermute x4, starting transfers between devices, passed_along(): lax.ppermute(value, axis, [(source, source + steps) for source in range(l...  12.8 us
    unnamed x45, local copies, waits for them, and re-layouts  7.74 us
    ppermute x4, local copies, waits for them, and re-layouts, from_behind(): return lax.ppermute(block, axis, route)  7.34 us
    squeeze x4, local copies, waits for them, and re-layouts, on_device(): results[0]  7.17 us
  transfers between devices with their start and end apart: 12, of which 6 were waited for; matrix products, arithmetic and copies ran while one was open for 7% of the time, Pallas kernels for 0%

commit v1 on v0

v1 whole, which is shorter than its diff:
```python
import functools

import jax
import jax.numpy as jnp
from jax import lax
from jax.experimental import pallas as pl
from jax.experimental.pallas import tpu as pltpu
from jax.sharding import PartitionSpec as P

STEPS = 2
SUB = 12
STRIP = 16
MESH = pl.DeviceIdType.MESH


def window_kernel(
    n, plan, s_ref, surface_in, flux_x_in, flux_y_in, celerity_in, bed_in, rough_in,
    level_out, held_out, got_out, energy_out,
    level, flux_x, flux_y, celerity, bed, rough, drag, turned, held, settled,
    below, above_level, above_flux, above_celerity, shares,
    load_sem, store_sem, send_sem, recv_sem, share_send, share_recv,
):
    rows, cols = flux_y.shape
    side = s_ref.shape[0]
    blocks = cols // side
    half = cols // 2
    me = lax.axis_index("tile")
    ahead_tile = lax.rem(me + 1, n)
    behind_tile = lax.rem(me + n - 1, n)
    top = me == 0
    bottom = me == n - 1
    f32, bf16 = jnp.float32, jnp.bfloat16

    loads = [
        pltpu.make_async_copy(source, target, load_sem.at[i])
        for i, (source, target) in enumerate(
            (
                (surface_in, level.at[pl.ds(0, rows)]),
                (celerity_in, celerity),
                (flux_x_in, flux_x.at[pl.ds(8, rows)]),
                (flux_y_in, flux_y),
                (bed_in, bed),
                (rough_in, rough),
            )
        )
    ]
    for load in loads:
        load.start()

    barrier = pltpu.get_barrier_semaphore()

    def greet(d, _):
        pl.semaphore_signal(barrier, inc=1, device_id={"tile": lax.rem(me + d, n)}, device_id_type=MESH)
        return 0

    lax.fori_loop(1, n, greet, 0)
    pl.semaphore_wait(barrier, n - 1)

    def remote(source, target, index, device):
        return pltpu.make_async_remote_copy(
            src_ref=source, dst_ref=target, send_sem=send_sem.at[index], recv_sem=recv_sem.at[index],
            device_id={"tile": device}, device_id_type=MESH,
        )

    last = pl.ds(rows - 8, 8)
    up = [
        remote(surface_in.at[pl.ds(0, 8)], below.at[0], 0, behind_tile),
        remote(level.at[pl.ds(0, 8)], below.at[1], 1, behind_tile),
    ]
    down = [
        [
            remote(surface_in.at[last], above_level.at[0], 2, ahead_tile),
            remote(flux_x_in.at[last], above_flux.at[0], 3, ahead_tile),
            remote(celerity_in.at[last], above_celerity, 4, ahead_tile),
        ],
        [
            remote(level.at[last], above_level.at[1], 5, ahead_tile),
            remote(flux_x.at[pl.ds(rows, 8)], above_flux.at[1], 6, ahead_tile),
        ],
    ]

    @pl.when(jnp.logical_not(top))
    def _():
        up[0].start()

    @pl.when(jnp.logical_not(bottom))
    def _():
        for copy in down[0]:
            copy.start()

    turned[...] = s_ref[...].astype(f32).T.astype(bf16)
    codes = [plan[0, c] for c in range(blocks)]

    def choose(options, matches):
        chosen = options[0]
        for option, match in zip(options[1:], matches[1:]):
            chosen = jnp.where(match, option, chosen)
        return chosen

    def with_code(wide, code):
        parts = [wide[:, c * side : (c + 1) * side] for c in range(blocks)]
        return choose(parts, [codes[c] == code for c in range(blocks)])

    def joined(which, at, size):
        options = [settled[code, which, pl.ds(at, size), :] for code in range(4)]
        return jnp.concatenate(
            [choose(options, [codes[c] == code for code in range(4)]) for c in range(blocks)], 1
        )

    col_ids = lax.broadcasted_iota(jnp.int32, (1, cols), 1)
    right_edge = lax.rem(col_ids, half) == half - 1
    left_edge = lax.rem(col_ids, half) == 0

    for load in loads:
        load.wait()

    def strip_flux(step, which, at):
        if step == 0:
            return flux_x[pl.ds(8 + at, STRIP)] if which == 0 else flux_y[pl.ds(at, STRIP)]
        return joined(which, at, STRIP)

    def advance(step):
        @pl.when(bottom)
        def _():
            level[pl.ds(rows, 8)] = jnp.zeros((8, cols), f32)

        @pl.when(jnp.logical_not(bottom))
        def _():
            up[step].wait_recv()
            level[pl.ds(rows, 8)] = below[step]

        @pl.when(top)
        def _():
            flux_x[pl.ds(0, 8)] = jnp.zeros((8, cols), f32)

        @pl.when(jnp.logical_not(top))
        def _():
            for copy in down[step]:
                copy.wait_recv()
            flux_x[pl.ds(0, 8)] = above_flux[step] - above_celerity[...] * (
                level[0:1] - above_level[step]
            )

        def strip(i, _):
            at = pl.multiple_of(i * STRIP, STRIP)
            now = level[pl.ds(at, STRIP)]
            after = level[pl.ds(at + STRIP, 8)]
            ahead = pltpu.roll(jnp.concatenate([now, after], 0), STRIP + 7, 0)[:STRIP]
            wave = celerity[pl.ds(at, STRIP)]
            new_x = strip_flux(step, 0, at) - wave * (ahead - now)
            right = jnp.where(right_edge, 0.0, pltpu.roll(now, cols - 1, 1))
            new_y = strip_flux(step, 1, at) - wave * (right - now)
            behind_x = pltpu.roll(jnp.concatenate([flux_x[pl.ds(at, 8)], new_x], 0), 1, 0)[8:]
            behind_y = jnp.where(left_edge, 0.0, pltpu.roll(new_y, 1, 1))
            new_level = now - (new_x - behind_x) - (new_y - behind_y)
            flux_x[pl.ds(8 + at, STRIP)] = new_x
            level[pl.ds(at, STRIP)] = new_level
            ratio = rough[pl.ds(at, STRIP)] / jnp.maximum(new_level + bed[pl.ds(at, STRIP)], 1.0)
            ratio = ratio.astype(bf16).astype(f32)
            for code in range(1, 4):
                drag[code - 1, pl.ds(at, STRIP), :] = with_code(ratio, code)
            for which, new in enumerate((new_x, new_y)):
                for code in range(4):
                    mine = with_code(new, code)
                    held[code, which, pl.ds(at, STRIP), :] = mine.astype(bf16)
                    if code == 0:
                        settled[0, which, pl.ds(at, STRIP), :] = mine
            return 0

        lax.fori_loop(0, rows // STRIP, strip, 0)

    def settle(wanted):
        def once(code, which):
            mixed = jnp.dot(held[code, which], turned[...], preferred_element_type=f32).astype(bf16)
            smoothed = jnp.dot(s_ref[...], mixed, preferred_element_type=f32)
            weight = drag[code - 1]
            return smoothed * pl.reciprocal(1.0 + weight * jnp.abs(smoothed), approx=True)

        def body(i, _):
            for code in wanted:
                for which in range(2):
                    held[code, which] = once(code, which).astype(bf16)
            return 0

        lax.fori_loop(0, SUB - 1, body, 0)
        for code in wanted:
            for which in range(2):
                value = once(code, which)
                settled[code, which] = value
                held[code, which] = value.astype(bf16)

    advance(0)
    for copy, edge in ((up[0], top), (down[0][0], bottom), (down[0][1], bottom), (down[0][2], bottom)):
        @pl.when(jnp.logical_not(edge))
        def _():
            copy.wait_send()

    @pl.when(jnp.logical_not(top))
    def _():
        up[1].start()

    @pl.when(jnp.logical_not(bottom))
    def _():
        down[1][0].start()

    settle((1, 2, 3))
    flux_x[pl.ds(rows, 8)] = joined(0, rows - 8, 8)

    @pl.when(jnp.logical_not(top))
    def _():
        up[1].wait_send()

    @pl.when(jnp.logical_not(bottom))
    def _():
        down[1][1].start()
        down[1][0].wait_send()
        down[1][1].wait_send()

    advance(1)

    total = n * rows

    def add_up(i, sums):
        at = pl.multiple_of(i * 8, 8)
        row = (me * rows + at + lax.broadcasted_iota(jnp.int32, (8, 1), 0)).astype(f32)
        value = level[pl.ds(at, 8)]
        return sums + (1.0 + 2.0 * row / total) * (value * value)

    sums = lax.fori_loop(0, rows // 8, add_up, jnp.zeros((8, cols), f32))
    for scenario in range(2):
        share = jnp.zeros((8, 128), f32)
        for c in range(half // 128):
            share = share + sums[:, scenario * half + c * 128 : scenario * half + (c + 1) * 128]
        shares[me, scenario] = share

    def spread(d, _):
        share_copy(d).start()
        return 0

    def share_copy(d):
        return pltpu.make_async_remote_copy(
            src_ref=shares.at[me], dst_ref=shares.at[me],
            send_sem=share_send.at[d - 1], recv_sem=share_recv.at[d - 1],
            device_id={"tile": lax.rem(me + d, n)}, device_id_type=MESH,
        )

    lax.fori_loop(1, n, spread, 0)
    keep_level = pltpu.make_async_copy(level.at[pl.ds(0, rows)], level_out, store_sem.at[0])
    keep_level.start()
    keep_dry = pltpu.make_async_copy(held.at[0], held_out.at[0], store_sem.at[4])
    keep_dry.start()

    sends = []
    keeps = [keep_dry]
    for code in (3, 2, 1):
        settle((code,))
        if code > 1:
            hop = code - 1
            send = remote(held.at[code], got_out.at[hop - 1], 6 + hop, lax.rem(me + hop, n))
            send.start()
            sends.append(send)
        keep = pltpu.make_async_copy(held.at[code], held_out.at[code], store_sem.at[code])
        keep.start()
        keeps.append(keep)

    def gather(d, _):
        share_copy(d).wait()
        return 0

    lax.fori_loop(1, n, gather, 0)
    for scenario in range(2):
        def add_share(d, value):
            return value + shares[d, scenario]

        whole = lax.fori_loop(0, n, add_share, jnp.zeros((8, 128), f32))
        energy_out[scenario] = jnp.sum(whole) / (total * half)
    keep_level.wait()
    for keep in keeps:
        keep.wait()
    for send in sends:
        send.wait()


def write_kernel(plan, level, held, got, level_out, flux_x_out, flux_y_out, resident_out):
    side = held.shape[-1]
    level_out[...] = level[...]
    for c in range(level.shape[1] // side):
        part = pl.ds(c * side, side)
        flux_x_out[:, part] = held[plan[0, c], 0].astype(jnp.float32)
        flux_y_out[:, part] = held[plan[0, c], 1].astype(jnp.float32)
    resident_out[0] = held[1].astype(jnp.float32)
    resident_out[1] = got[0].astype(jnp.float32)
    resident_out[2] = got[1].astype(jnp.float32)


def on_device(surface, flux_x, flux_y, celerity, bed_depth, roughness, smoother, block_plan):
    rows, cols = surface.shape
    side = smoother.shape[0]
    n = lax.axis_size("tile")
    f32, bf16 = jnp.float32, jnp.bfloat16
    whole = pl.BlockSpec(memory_space=pl.ANY)
    smem = pl.BlockSpec(memory_space=pltpu.SMEM)
    vmem = pl.BlockSpec(memory_space=pltpu.VMEM)
    level, held, got, energy = pl.pallas_call(
        functools.partial(window_kernel, n),
        out_shape=(
            jax.ShapeDtypeStruct((rows, cols), f32),
            jax.ShapeDtypeStruct((4, 2, side, side), bf16),
            jax.ShapeDtypeStruct((2, 2, side, side), bf16),
            jax.ShapeDtypeStruct((2,), f32),
        ),
        in_specs=[smem, vmem] + [whole] * 6,
        out_specs=(whole, whole, whole, smem),
        scratch_shapes=[
            pltpu.VMEM((rows + 8, cols), f32),
            pltpu.VMEM((rows + 8, cols), f32),
            pltpu.VMEM((rows, cols), f32),
            pltpu.VMEM((rows, cols), f32),
            pltpu.VMEM((rows, cols), f32),
            pltpu.VMEM((rows, cols), f32),
            pltpu.VMEM((3, side, side), f32),
            pltpu.VMEM((side, side), bf16),
            pltpu.VMEM((4, 2, side, side), bf16),
            pltpu.VMEM((4, 2, side, side), f32),
            pltpu.VMEM((2, 8, cols), f32),
            pltpu.VMEM((2, 8, cols), f32),
            pltpu.VMEM((2, 8, cols), f32),
            pltpu.VMEM((8, cols), f32),
            pltpu.VMEM((n, 2, 8, 128), f32),
            pltpu.SemaphoreType.DMA((6,)),
            pltpu.SemaphoreType.DMA((5,)),
            pltpu.SemaphoreType.DMA((9,)),
            pltpu.SemaphoreType.DMA((9,)),
            pltpu.SemaphoreType.DMA((n - 1,)),
            pltpu.SemaphoreType.DMA((n - 1,)),
        ],
        compiler_params=pltpu.CompilerParams(
            collective_id=0, has_side_effects=True, vmem_limit_bytes=40 * 1024 * 1024
        ),
        name="window",
    )(block_plan, smoother, surface, flux_x, flux_y, celerity, bed_depth, roughness)

    step = 64
    flat = pl.BlockSpec((step, cols), lambda i: (i, 0))
    new_surface, new_x, new_y, resident = pl.pallas_call(
        write_kernel,
        grid=(rows // step,),
        out_shape=(
            jax.ShapeDtypeStruct((rows, cols), f32),
            jax.ShapeDtypeStruct((rows, cols), f32),
            jax.ShapeDtypeStruct((rows, cols), f32),
            jax.ShapeDtypeStruct((3, 2, side, side), f32),
        ),
        in_specs=[
            smem,
            flat,
            pl.BlockSpec((4, 2, step, side), lambda i: (0, 0, i, 0)),
            pl.BlockSpec((2, 2, step, side), lambda i: (0, 0, i, 0)),
        ],
        out_specs=(flat, flat, flat, pl.BlockSpec((3, 2, step, side), lambda i: (0, 0, i, 0))),
        compiler_params=pltpu.CompilerParams(vmem_limit_bytes=20 * 1024 * 1024),
        name="write_out",
    )(block_plan, level, held, got)
    return new_surface, new_x, new_y, resident, energy


def solution(mesh):
    fields = P(("ens", "tile"), None)
    return jax.shard_map(
        on_device,
        mesh=mesh,
        in_specs=(fields,) * 6 + (P(), fields),
        out_specs=(fields, fields, fields, P(("ens", "tile"), None, None, None), P("ens")),
        check_vma=False,
    )
```

time: 197 us -> 56.8 us (0.29)
  matrix products: 59.5 us -> 0 us
  Pallas kernels: 0 us -> 46.3 us
  waiting for transfers between devices: 33.3 us -> 0 us
  blocking collectives: 29.1 us -> 0 us
  starting transfers between devices: 27.1 us -> 0 us
  local copies, waits for them, and re-layouts: 30.5 us -> 9.41 us
  other arithmetic: 14.6 us -> 0 us
    dot_general x24 -> x0, matrix products: 59.5 us -> none  [soften(): jnp.einsum('ki,sfij->sfkj', smoother, partial_rows, preferred_element_typ...]
    pallas_call x0 -> x2, Pallas kernels: none -> 46.3 us  [the longest x1 43.1 us: on_device(): pl.pallas_call(functools.partial(window_kernel, n), out_shape=(jax.ShapeD...]
    ppermute x12 -> x0, waiting for transfers between devices: 33.3 us -> none  [the longest x8 33.3 us: from_behind(): return lax.ppermute(block, axis, route)]
    psum x1 -> x0, blocking collectives: 29.1 us -> none  [on_device(): energy = lax.psum(term_pair, 'tile')]
    ppermute x12 -> x0, starting transfers between devices: 27.1 us -> none  [the longest x8 14.2 us: from_behind(): return lax.ppermute(block, axis, route)]
    squeeze x6 -> x0, local copies, waits for them, and re-layouts: 7.45 us -> none  [the longest x4 7.17 us: on_device(): results[0]]
    ppermute x4 -> x0, local copies, waits for them, and re-layouts: 7.34 us -> none  [from_behind(): return lax.ppermute(block, axis, route)]
    slice x13 -> x0, local copies, waits for them, and re-layouts: 5.63 us -> none  [the longest x2 2.39 us: on_device(): ahead_rows = jnp.concatenate([level[1:], below_row], 0)]
  transfers between devices with their start and end apart: 12 -> 0, of which waited for: 6 -> 0; matrix products, arithmetic and copies ran while one was open for 7% -> 0% of each run, Pallas kernels for 0% -> 0%
where the time goes in v1:
time: 56.8 us; the launch traced here: 56.4 us
  Pallas kernels  46.3 us (82%)
  local copies, waits for them, and re-layouts  9.41 us (17%)
  between operations  0.66 us (1%)
    pallas_call x1, Pallas kernels, on_device(): pl.pallas_call(functools.partial(window_kernel, n), out_shape=(jax.ShapeD...  43.1 us
    unnamed x17, local copies, waits for them, and re-layouts  9.41 us
    pallas_call x1, Pallas kernels, on_device(): pl.pallas_call(write_kernel, grid=(rows // step,), out_shape=(jax.ShapeDt...  3.16 us

profile of v1, /device:TPU:0, one launch (start us, length us, event | category | flops | bytes accessed | tf_op | source)
XLA Modules:
  0.0 56.4 jit_solution(9290702970122527972)
XLA Ops:
  0.6 0.0 copy-start
  0.6 1.2 %copy-done = f32[256,1024]{1,0:T(8,128)S(1)} copy-done((f32[256,1024]{1,0:T(8,128)S(1)}, f32[256,1024]{1,0:T(8,128)}, u32[]{:S(2)}) %copy-start) | copy-done | bytes 1048600
  1.9 0.0 copy-start.1
  1.9 1.2 %copy-done.1 = f32[256,1024]{1,0:T(8,128)S(1)} copy-done((f32[256,1024]{1,0:T(8,128)S(1)}, f32[256,1024]{1,0:T(8,128)}, u32[]{:S(2)}) %copy-start.1) | copy-done | bytes 1048600
  3.1 0.0 copy-start.2
  3.1 1.2 %copy-done.2 = f32[256,1024]{1,0:T(8,128)S(1)} copy-done((f32[256,1024]{1,0:T(8,128)S(1)}, f32[256,1024]{1,0:T(8,128)}, u32[]{:S(2)}) %copy-start.2) | copy-done | bytes 1048600
  4.3 0.0 copy-start.3
  4.3 1.2 %copy-done.3 = f32[256,1024]{1,0:T(8,128)S(1)} copy-done((f32[256,1024]{1,0:T(8,128)S(1)}, f32[256,1024]{1,0:T(8,128)}, u32[]{:S(2)}) %copy-start.3) | copy-done | bytes 1048600
  5.5 0.0 copy-start.4
  5.5 1.2 %copy-done.4 = f32[256,1024]{1,0:T(8,128)S(1)} copy-done((f32[256,1024]{1,0:T(8,128)S(1)}, f32[256,1024]{1,0:T(8,128)}, u32[]{:S(2)}) %copy-start.4) | copy-done | bytes 1048600
  6.8 0.0 copy-start.5
  6.8 1.2 %copy-done.5 = f32[256,1024]{1,0:T(8,128)S(1)} copy-done((f32[256,1024]{1,0:T(8,128)S(1)}, f32[256,1024]{1,0:T(8,128)}, u32[]{:S(2)}) %copy-start.5) | copy-done | bytes 1048600
  8.0 0.0 copy-start.6
  8.0 0.9 %copy-done.6 = bf16[256,256]{1,0:T(8,128)(2,1)S(1)} copy-done((bf16[256,256]{1,0:T(8,128)(2,1)S(1)}, bf16[256,256]{1,0:T(8,128)(2,1)}, u32[]{:S(2)}) %copy-start.6) | copy-done | bytes 131096
  8.9 0.0 copy-start.7
  8.9 0.7 %copy-done.7 = s32[1,4]{1,0:T(1,128)S(1)} copy-done((s32[1,4]{1,0:T(1,128)S(1)}, s32[1,4]{1,0:T(1,128)}, u32[]{:S(2)}) %copy-start.7) | copy-done | bytes 40
  9.5 43.1 %window.1 = (f32[256,1024]{1,0:T(8,128)S(1)}, bf16[4,2,256,256]{3,2,1,0:T(8,128)(2,1)S(1)}, bf16[2,2,256,256]{3,2,1,0:T(8,128)(2,1)S(1)}, f32[2]{0:T(128)S(1)}) custom-call(s32[1,4]{1,0:T(1,128)S(1)} %copy-done.7, bf16[256,256]{1,0:T(8,128)(2,1)S(1)} %copy-done.6, f32[256,1024]{1,0:T(8,128)S(1)} %copy-done, f32[256,1024]{1,0:T(8,128)S(1)} %copy-done.1, ...), custom_call_target="tpu_custom_call" | custom-call | tf_op jit(solution)/shard_map/window/pallas_call | solution.py:304
  52.7 3.2 %write_out.1 = (f32[256,1024]{1,0:T(8,128)}, f32[256,1024]{1,0:T(8,128)}, f32[256,1024]{1,0:T(8,128)}, f32[3,2,256,256]{3,2,1,0:T(8,128)}) custom-call(s32[1,4]{1,0:T(1,128)S(1)} %copy-done.7, f32[256,1024]{1,0:T(8,128)S(1)} %get-tuple-element.13.level, bf16[4,2,256,256]{3,2,1,0:T(8,128)(2,1)S(1)} %get-tuple-element.14.held, ...), custom_call_target="tpu_custom_call" | custom-call | tf_op jit(solution)/shard_map/write_out/pallas_call | solution.py:345
  55.9 0.5 copy.14
Async XLA Ops:
  0.6 1.2 %copy-start = (f32[256,1024]{1,0:T(8,128)S(1)}, f32[256,1024]{1,0:T(8,128)}, u32[]{:S(2)}) copy-start(f32[256,1024]{1,0:T(8,128)} %surface_in.1) | copy-start | bytes 3145732
  1.9 1.2 %copy-start.1 = (f32[256,1024]{1,0:T(8,128)S(1)}, f32[256,1024]{1,0:T(8,128)}, u32[]{:S(2)}) copy-start(f32[256,1024]{1,0:T(8,128)} %flux_x_in.1) | copy-start | bytes 3145732
  3.1 1.2 %copy-start.2 = (f32[256,1024]{1,0:T(8,128)S(1)}, f32[256,1024]{1,0:T(8,128)}, u32[]{:S(2)}) copy-start(f32[256,1024]{1,0:T(8,128)} %flux_y_in.1) | copy-start | bytes 3145732
  4.3 1.2 %copy-start.3 = (f32[256,1024]{1,0:T(8,128)S(1)}, f32[256,1024]{1,0:T(8,128)}, u32[]{:S(2)}) copy-start(f32[256,1024]{1,0:T(8,128)} %celerity_in.1) | copy-start | bytes 3145732
  5.5 1.2 %copy-start.4 = (f32[256,1024]{1,0:T(8,128)S(1)}, f32[256,1024]{1,0:T(8,128)}, u32[]{:S(2)}) copy-start(f32[256,1024]{1,0:T(8,128)} %bed_in.1) | copy-start | bytes 3145732
  6.8 1.2 %copy-start.5 = (f32[256,1024]{1,0:T(8,128)S(1)}, f32[256,1024]{1,0:T(8,128)}, u32[]{:S(2)}) copy-start(f32[256,1024]{1,0:T(8,128)} %rough_in.1) | copy-start | bytes 3145732
  8.0 0.9 %copy-start.6 = (bf16[256,256]{1,0:T(8,128)(2,1)S(1)}, bf16[256,256]{1,0:T(8,128)(2,1)}, u32[]{:S(2)}) copy-start(bf16[256,256]{1,0:T(8,128)(2,1)} %s_ref.1) | copy-start | bytes 393220
  8.9 0.7 %copy-start.7 = (s32[1,4]{1,0:T(1,128)S(1)}, s32[1,4]{1,0:T(1,128)}, u32[]{:S(2)}) copy-start(s32[1,4]{1,0:T(1,128)} %plan.3) | copy-start | bytes 52

commit v2 on v1

--- a/solution.py
+++ b/solution.py
@@ -14,11 +14,11 @@
 
 
 def window_kernel(
-    n, plan, s_ref, surface_in, flux_x_in, flux_y_in, celerity_in, bed_in, rough_in,
+    n, plan_in, smoother_in, surface_in, flux_x_in, flux_y_in, celerity_in, bed_in, rough_in,
     level_out, held_out, got_out, energy_out,
     level, flux_x, flux_y, celerity, bed, rough, drag, turned, held, settled,
     below, above_level, above_flux, above_celerity, shares,
-    load_sem, store_sem, send_sem, recv_sem, share_send, share_recv,
+    plan, s_ref, load_sem, store_sem, send_sem, recv_sem, share_send, share_recv,
 ):
     rows, cols = flux_y.shape
     side = s_ref.shape[0]
@@ -41,6 +41,8 @@
                 (flux_y_in, flux_y),
                 (bed_in, bed),
                 (rough_in, rough),
+                (smoother_in, s_ref),
+                (plan_in, plan),
             )
         )
     ]
@@ -88,6 +90,8 @@
         for copy in down[0]:
             copy.start()
 
+    for load in loads:
+        load.wait()
     turned[...] = s_ref[...].astype(f32).T.astype(bf16)
     codes = [plan[0, c] for c in range(blocks)]
 
@@ -110,9 +114,6 @@
     col_ids = lax.broadcasted_iota(jnp.int32, (1, cols), 1)
     right_edge = lax.rem(col_ids, half) == half - 1
     left_edge = lax.rem(col_ids, half) == 0
-
-    for load in loads:
-        load.wait()
 
     def strip_flux(step, which, at):
         if step == 0:
@@ -158,7 +159,7 @@
             ratio = rough[pl.ds(at, STRIP)] / jnp.maximum(new_level + bed[pl.ds(at, STRIP)], 1.0)
             ratio = ratio.astype(bf16).astype(f32)
             for code in range(1, 4):
-                drag[code - 1, pl.ds(at, STRIP), :] = with_code(ratio, code)
+                drag[0, code - 1, pl.ds(at, STRIP), :] = with_code(ratio, code)
             for which, new in enumerate((new_x, new_y)):
                 for code in range(4):
                     mine = with_code(new, code)
@@ -170,24 +171,40 @@
         lax.fori_loop(0, rows // STRIP, strip, 0)
 
     def settle(wanted):
-        def once(code, which):
-            mixed = jnp.dot(held[code, which], turned[...], preferred_element_type=f32).astype(bf16)
-            smoothed = jnp.dot(s_ref[...], mixed, preferred_element_type=f32)
-            weight = drag[code - 1]
-            return smoothed * pl.reciprocal(1.0 + weight * jnp.abs(smoothed), approx=True)
+        def product(pieces):
+            tall = jnp.dot(
+                jnp.concatenate(pieces, 0), turned[...], preferred_element_type=f32
+            )
+            return [tall[i * side : (i + 1) * side] for i in range(len(pieces))]
+
+        def once(flip):
+            pieces = [held[code, which] for code in wanted for which in range(2)]
+            mixed = [piece.astype(bf16).T for piece in product(pieces)]
+            smoothed = product(mixed)
+            out = []
+            for i, value in enumerate(smoothed):
+                weight = drag[flip, wanted[i // 2] - 1]
+                out.append(value * pl.reciprocal(1.0 + weight * jnp.abs(value), approx=True))
+            return out
+
+        def keep_bf16(values):
+            for i, value in enumerate(values):
+                held[wanted[i // 2], i % 2] = value.astype(bf16)
+
+        for code in wanted:
+            drag[1, code - 1] = drag[0, code - 1].T
 
         def body(i, _):
-            for code in wanted:
-                for which in range(2):
-                    held[code, which] = once(code, which).astype(bf16)
+            keep_bf16(once(1))
+            keep_bf16(once(0))
             return 0
 
-        lax.fori_loop(0, SUB - 1, body, 0)
-        for code in wanted:
-            for which in range(2):
-                value = once(code, which)
-                settled[code, which] = value
-                held[code, which] = value.astype(bf16)
+        lax.fori_loop(0, SUB // 2 - 1, body, 0)
+        keep_bf16(once(1))
+        values = once(0)
+        keep_bf16(values)
+        for i, value in enumerate(values):
+            settled[wanted[i // 2], i % 2] = value
 
     advance(0)
     for copy, edge in ((up[0], top), (down[0][0], bottom), (down[0][1], bottom), (down[0][2], bottom)):
@@ -298,9 +315,8 @@
     side = smoother.shape[0]
     n = lax.axis_size("tile")
     f32, bf16 = jnp.float32, jnp.bfloat16
-    whole = pl.BlockSpec(memory_space=pl.ANY)
+    whole = pl.BlockSpec(memory_space=pltpu.HBM)
     smem = pl.BlockSpec(memory_space=pltpu.SMEM)
-    vmem = pl.BlockSpec(memory_space=pltpu.VMEM)
     level, held, got, energy = pl.pallas_call(
         functools.partial(window_kernel, n),
         out_shape=(
@@ -309,7 +325,7 @@
             jax.ShapeDtypeStruct((2, 2, side, side), bf16),
             jax.ShapeDtypeStruct((2,), f32),
         ),
-        in_specs=[smem, vmem] + [whole] * 6,
+        in_specs=[whole] * 8,
         out_specs=(whole, whole, whole, smem),
         scratch_shapes=[
             pltpu.VMEM((rows + 8, cols), f32),
@@ -318,7 +334,7 @@
             pltpu.VMEM((rows, cols), f32),
             pltpu.VMEM((rows, cols), f32),
             pltpu.VMEM((rows, cols), f32),
-            pltpu.VMEM((3, side, side), f32),
+            pltpu.VMEM((2, 3, side, side), f32),
             pltpu.VMEM((side, side), bf16),
             pltpu.VMEM((4, 2, side, side), bf16),
             pltpu.VMEM((4, 2, side, side), f32),
@@ -327,7 +343,9 @@
             pltpu.VMEM((2, 8, cols), f32),
             pltpu.VMEM((8, cols), f32),
             pltpu.VMEM((n, 2, 8, 128), f32),
-            pltpu.SemaphoreType.DMA((6,)),
+            pltpu.SMEM(block_plan.shape, jnp.int32),
+            pltpu.VMEM((side, side), bf16),
+            pltpu.SemaphoreType.DMA((8,)),
             pltpu.SemaphoreType.DMA((5,)),
             pltpu.SemaphoreType.DMA((9,)),
             pltpu.SemaphoreType.DMA((9,)),
@@ -335,7 +353,7 @@
             pltpu.SemaphoreType.DMA((n - 1,)),
         ],
         compiler_params=pltpu.CompilerParams(
-            collective_id=0, has_side_effects=True, vmem_limit_bytes=40 * 1024 * 1024
+            collective_id=0, has_side_effects=True, vmem_limit_bytes=56 * 1024 * 1024
         ),
         name="window",
     )(block_plan, smoother, surface, flux_x, flux_y, celerity, bed_depth, roughness)

time: 56.8 us -> 48.2 us (0.85)
  local copies, waits for them, and re-layouts: 9.41 us -> 4 us
  Pallas kernels: 46.3 us -> 43.3 us
    unnamed x17 -> x11, local copies, waits for them, and re-layouts: 9.41 us -> 4 us
    pallas_call x1, Pallas kernels: 43.1 us -> 40.2 us  [on_device(): pl.pallas_call(functools.partial(window_kernel, n), out_shape=(jax.ShapeD...]
where the time goes in v2:
time: 48.2 us; the launch traced here: 48 us
  Pallas kernels  43.3 us (90%)
  local copies, waits for them, and re-layouts  4 us (8%)
  between operations  0.68 us (1%)
    pallas_call x1, Pallas kernels, on_device(): pl.pallas_call(functools.partial(window_kernel, n), out_shape=(jax.ShapeD...  40.2 us
    unnamed x11, local copies, waits for them, and re-layouts  4 us
    pallas_call x1, Pallas kernels, on_device(): pl.pallas_call(write_kernel, grid=(rows // step,), out_shape=(jax.ShapeDt...  3.14 us

profile of v2, /device:TPU:0, one launch (start us, length us, event | category | flops | bytes accessed | tf_op | source)
XLA Modules:
  0.0 48.0 jit_solution(12207242704558690034)
XLA Ops:
  0.6 0.0 copy-start.3
  0.6 40.2 %window.1 = (f32[256,1024]{1,0:T(8,128)}, bf16[4,2,256,256]{3,2,1,0:T(8,128)(2,1)}, bf16[2,2,256,256]{3,2,1,0:T(8,128)(2,1)}, f32[2]{0:T(128)}) custom-call(s32[1,4]{1,0:T(1,128)} %plan.1, bf16[256,256]{1,0:T(8,128)(2,1)} %smoother_in.1, f32[256,1024]{1,0:T(8,128)} %surface_in.1, f32[256,1024]{1,0:T(8,128)} %flux_x_in.1, f32[256,1024]{1,0:T(8,128)} %flux_y_in.1, ...), custom_call_target="tpu_custom_call" | custom-call | tf_op jit(solution)/shard_map/window/pallas_call | solution.py:320
  40.8 0.0 copy-start.4
  40.8 0.0 copy-done.3
  40.8 0.0 copy-start
  40.8 1.2 %copy-done = f32[256,1024]{1,0:T(8,128)S(1)} copy-done((f32[256,1024]{1,0:T(8,128)S(1)}, f32[256,1024]{1,0:T(8,128)}, u32[]{:S(2)}) %copy-start) | copy-done | bytes 1048600
  42.1 0.0 copy-start.1
  42.1 1.2 %copy-done.1 = bf16[4,2,256,256]{3,2,1,0:T(8,128)(2,1)S(1)} copy-done((bf16[4,2,256,256]{3,2,1,0:T(8,128)(2,1)S(1)}, bf16[4,2,256,256]{3,2,1,0:T(8,128)(2,1)}, u32[]{:S(2)}) %copy-start.1) | copy-done | bytes 1048600
  43.3 0.0 copy-start.2
  43.3 1.0 %copy-done.2 = bf16[2,2,256,256]{3,2,1,0:T(8,128)(2,1)S(1)} copy-done((bf16[2,2,256,256]{3,2,1,0:T(8,128)(2,1)S(1)}, bf16[2,2,256,256]{3,2,1,0:T(8,128)(2,1)}, u32[]{:S(2)}) %copy-start.2) | copy-done | bytes 524312
  44.3 3.1 %write_out.1 = (f32[256,1024]{1,0:T(8,128)}, f32[256,1024]{1,0:T(8,128)}, f32[256,1024]{1,0:T(8,128)}, f32[3,2,256,256]{3,2,1,0:T(8,128)}) custom-call(s32[1,4]{1,0:T(1,128)S(1)} %copy-done.3, f32[256,1024]{1,0:T(8,128)S(1)} %copy-done, bf16[4,2,256,256]{3,2,1,0:T(8,128)(2,1)S(1)} %copy-done.1, bf16[2,2,256,256]{3,2,1,0:T(8,128)(2,1)S(1)} %copy-done.2), custom_call_target="tpu_custom_call" | custom-call | tf_op jit(solution)/shard_map/write_out/pallas_call | solution.py:363
  47.5 0.0 copy-done.4
  47.5 0.5 %copy.14 = f32[2]{0:T(128)} copy(f32[2]{0:T(128)S(1)} %copy-done.4) | data formatting | bytes 16
Async XLA Ops:
  0.6 40.2 %copy-start.3 = (s32[1,4]{1,0:T(1,128)S(1)}, s32[1,4]{1,0:T(1,128)}, u32[]{:S(2)}) copy-start(s32[1,4]{1,0:T(1,128)} %plan.1) | copy-start | bytes 52
  40.8 6.7 %copy-start.4 = (f32[2]{0:T(128)S(1)}, f32[2]{0:T(128)}, u32[]{:S(2)}) copy-start(f32[2]{0:T(128)} %get-tuple-element.30) | copy-start | bytes 28
  40.8 1.2 %copy-start = (f32[256,1024]{1,0:T(8,128)S(1)}, f32[256,1024]{1,0:T(8,128)}, u32[]{:S(2)}) copy-start(f32[256,1024]{1,0:T(8,128)} %get-tuple-element.13.level) | copy-start | bytes 3145732
  42.1 1.2 %copy-start.1 = (bf16[4,2,256,256]{3,2,1,0:T(8,128)(2,1)S(1)}, bf16[4,2,256,256]{3,2,1,0:T(8,128)(2,1)}, u32[]{:S(2)}) copy-start(bf16[4,2,256,256]{3,2,1,0:T(8,128)(2,1)} %get-tuple-element.14.held) | copy-start | bytes 3145732
  43.3 1.0 %copy-start.2 = (bf16[2,2,256,256]{3,2,1,0:T(8,128)(2,1)S(1)}, bf16[2,2,256,256]{3,2,1,0:T(8,128)(2,1)}, u32[]{:S(2)}) copy-start(bf16[2,2,256,256]{3,2,1,0:T(8,128)(2,1)} %get-tuple-element.15.got) | copy-start | bytes 1572868

commit v3 on v2

--- a/solution.py
+++ b/solution.py
@@ -178,20 +178,20 @@
             return [tall[i * side : (i + 1) * side] for i in range(len(pieces))]
 
         def once(flip):
-            pieces = [held[code, which] for code in wanted for which in range(2)]
+            pieces = [held[code, which] for code, which in wanted]
             mixed = [piece.astype(bf16).T for piece in product(pieces)]
             smoothed = product(mixed)
             out = []
             for i, value in enumerate(smoothed):
-                weight = drag[flip, wanted[i // 2] - 1]
+                weight = drag[flip, wanted[i][0] - 1]
                 out.append(value * pl.reciprocal(1.0 + weight * jnp.abs(value), approx=True))
             return out
 
         def keep_bf16(values):
             for i, value in enumerate(values):
-                held[wanted[i // 2], i % 2] = value.astype(bf16)
-
-        for code in wanted:
+                held[wanted[i]] = value.astype(bf16)
+
+        for code in sorted({code for code, _ in wanted}):
             drag[1, code - 1] = drag[0, code - 1].T
 
         def body(i, _):
@@ -204,7 +204,7 @@
         values = once(0)
         keep_bf16(values)
         for i, value in enumerate(values):
-            settled[wanted[i // 2], i % 2] = value
+            settled[wanted[i]] = value
 
     advance(0)
     for copy, edge in ((up[0], top), (down[0][0], bottom), (down[0][1], bottom), (down[0][2], bottom)):
@@ -220,7 +220,7 @@
     def _():
         down[1][0].start()
 
-    settle((1, 2, 3))
+    settle([(code, which) for code in (1, 2, 3) for which in range(2)])
     flux_x[pl.ds(rows, 8)] = joined(0, rows - 8, 8)
 
     @pl.when(jnp.logical_not(top))
@@ -269,16 +269,18 @@
 
     sends = []
     keeps = [keep_dry]
-    for code in (3, 2, 1):
-        settle((code,))
-        if code > 1:
-            hop = code - 1
-            send = remote(held.at[code], got_out.at[hop - 1], 6 + hop, lax.rem(me + hop, n))
-            send.start()
-            sends.append(send)
+    for code in (3, 2):
+        settle([(code, 0), (code, 1), (1, 3 - code)])
+        hop = code - 1
+        send = remote(held.at[code], got_out.at[hop - 1], 6 + hop, lax.rem(me + hop, n))
+        send.start()
+        sends.append(send)
         keep = pltpu.make_async_copy(held.at[code], held_out.at[code], store_sem.at[code])
         keep.start()
         keeps.append(keep)
+    keep = pltpu.make_async_copy(held.at[1], held_out.at[1], store_sem.at[1])
+    keep.start()
+    keeps.append(keep)
 
     def gather(d, _):
         share_copy(d).wait()
@@ -376,7 +378,7 @@
             pl.BlockSpec((2, 2, step, side), lambda i: (0, 0, i, 0)),
         ],
         out_specs=(flat, flat, flat, pl.BlockSpec((3, 2, step, side), lambda i: (0, 0, i, 0))),
-        compiler_params=pltpu.CompilerParams(vmem_limit_bytes=20 * 1024 * 1024),
+        compiler_params=pltpu.CompilerParams(vmem_limit_bytes=56 * 1024 * 1024),
         name="write_out",
     )(block_plan, level, held, got)
     return new_surface, new_x, new_y, resident, energy

time: 48.2 us -> 46.5 us (0.965)
  local copies, waits for them, and re-layouts: 4 us -> 0.52 us
  Pallas kernels: 43.3 us -> 45.1 us
    unnamed x11 -> x3, local copies, waits for them, and re-layouts: 4 us -> 0.52 us
    pallas_call x1, Pallas kernels: 3.14 us -> 4.35 us  [on_device(): pl.pallas_call(write_kernel, grid=(rows // step,), out_shape=(jax.ShapeDt...]
    pallas_call x1, Pallas kernels: 40.2 us -> 40.8 us  [on_device(): pl.pallas_call(functools.partial(window_kernel, n), out_shape=(jax.ShapeD...]
where the time goes in v3:
time: 46.5 us; the launch traced here: 46.3 us
  Pallas kernels  45.1 us (97%)
  between operations  0.65 us (1%)
  local copies, waits for them, and re-layouts  0.52 us (1%)
    pallas_call x1, Pallas kernels, on_device(): pl.pallas_call(functools.partial(window_kernel, n), out_shape=(jax.ShapeD...  40.8 us
    pallas_call x1, Pallas kernels, on_device(): pl.pallas_call(write_kernel, grid=(rows // step,), out_shape=(jax.ShapeDt...  4.35 us

profile of v3, /device:TPU:0, one launch (start us, length us, event | category | flops | bytes accessed | tf_op | source)
XLA Modules:
  0.0 46.3 jit_solution(5946601583196582738)
XLA Ops:
  0.6 40.8 %window.1 = (f32[256,1024]{1,0:T(8,128)}, bf16[4,2,256,256]{3,2,1,0:T(8,128)(2,1)}, bf16[2,2,256,256]{3,2,1,0:T(8,128)(2,1)}, f32[2]{0:T(128)}) custom-call(s32[1,4]{1,0:T(1,128)} %plan.1, bf16[256,256]{1,0:T(8,128)(2,1)} %smoother_in.1, f32[256,1024]{1,0:T(8,128)} %surface_in.1, f32[256,1024]{1,0:T(8,128)} %flux_x_in.1, f32[256,1024]{1,0:T(8,128)} %flux_y_in.1, ...), custom_call_target="tpu_custom_call" | custom-call | tf_op jit(solution)/shard_map/window/pallas_call | solution.py:322
  41.4 0.0 copy-start
  41.4 4.3 %write_out.1 = (f32[256,1024]{1,0:T(8,128)}, f32[256,1024]{1,0:T(8,128)}, f32[256,1024]{1,0:T(8,128)}, f32[3,2,256,256]{3,2,1,0:T(8,128)}) custom-call(s32[1,4]{1,0:T(1,128)} %plan.1, f32[256,1024]{1,0:T(8,128)} %get-tuple-element.13.level, bf16[4,2,256,256]{3,2,1,0:T(8,128)(2,1)} %get-tuple-element.14.held, bf16[2,2,256,256]{3,2,1,0:T(8,128)(2,1)} %get-tuple-element.15.got), custom_call_target="tpu_custom_call" | custom-call | tf_op jit(solution)/shard_map/write_out/pallas_call | solution.py:365
  45.8 0.0 copy-done
  45.8 0.5 %copy.14 = f32[2]{0:T(128)} copy(f32[2]{0:T(128)S(1)} %copy-done) | data formatting | bytes 16
Async XLA Ops:
  41.4 4.4 %copy-start = (f32[2]{0:T(128)S(1)}, f32[2]{0:T(128)}, u32[]{:S(2)}) copy-start(f32[2]{0:T(128)} %get-tuple-element.30) | copy-start | bytes 28

commit v4 on v3

--- a/solution.py
+++ b/solution.py
@@ -17,7 +17,7 @@
     n, plan_in, smoother_in, surface_in, flux_x_in, flux_y_in, celerity_in, bed_in, rough_in,
     level_out, held_out, got_out, energy_out,
     level, flux_x, flux_y, celerity, bed, rough, drag, turned, held, settled,
-    below, above_level, above_flux, above_celerity, shares,
+    below, above_level, above_flux, above_celerity, rim, shares,
     plan, s_ref, load_sem, store_sem, send_sem, recv_sem, share_send, share_recv,
 ):
     rows, cols = flux_y.shape
@@ -31,23 +31,31 @@
     bottom = me == n - 1
     f32, bf16 = jnp.float32, jnp.bfloat16
 
+    cut = rows // 2
+    sources = (
+        (surface_in, level, 0),
+        (celerity_in, celerity, 0),
+        (flux_x_in, flux_x, 8),
+        (flux_y_in, flux_y, 0),
+        (bed_in, bed, 0),
+        (rough_in, rough, 0),
+    )
     loads = [
-        pltpu.make_async_copy(source, target, load_sem.at[i])
-        for i, (source, target) in enumerate(
-            (
-                (surface_in, level.at[pl.ds(0, rows)]),
-                (celerity_in, celerity),
-                (flux_x_in, flux_x.at[pl.ds(8, rows)]),
-                (flux_y_in, flux_y),
-                (bed_in, bed),
-                (rough_in, rough),
-                (smoother_in, s_ref),
-                (plan_in, plan),
+        [
+            pltpu.make_async_copy(
+                source.at[pl.ds(part * cut, cut)], target.at[pl.ds(lead + part * cut, cut)], load_sem.at[part, i]
             )
-        )
+            for i, (source, target, lead) in enumerate(sources)
+        ]
+        for part in range(2)
     ]
-    for load in loads:
-        load.start()
+    loads[0] += [
+        pltpu.make_async_copy(smoother_in, s_ref, load_sem.at[0, 6]),
+        pltpu.make_async_copy(plan_in, plan, load_sem.at[0, 7]),
+    ]
+    for part in range(2):
+        for load in loads[part]:
+            load.start()
 
     barrier = pltpu.get_barrier_semaphore()
 
@@ -77,7 +85,7 @@
         ],
         [
             remote(level.at[last], above_level.at[1], 5, ahead_tile),
-            remote(flux_x.at[pl.ds(rows, 8)], above_flux.at[1], 6, ahead_tile),
+            remote(rim, above_flux.at[1], 6, ahead_tile),
         ],
     ]
 
@@ -90,7 +98,7 @@
         for copy in down[0]:
             copy.start()
 
-    for load in loads:
+    for load in loads[0]:
         load.wait()
     turned[...] = s_ref[...].astype(f32).T.astype(bf16)
     codes = [plan[0, c] for c in range(blocks)]
@@ -120,27 +128,15 @@
             return flux_x[pl.ds(8 + at, STRIP)] if which == 0 else flux_y[pl.ds(at, STRIP)]
         return joined(which, at, STRIP)
 
+    def drag_of(at, new_level):
+        ratio = rough[pl.ds(at, STRIP)] / jnp.maximum(new_level + bed[pl.ds(at, STRIP)], 1.0)
+        ratio = ratio.astype(bf16)
+        for code in range(1, 4):
+            drag[0, code - 1, pl.ds(at, STRIP), :] = with_code(ratio, code)
+
     def advance(step):
-        @pl.when(bottom)
-        def _():
-            level[pl.ds(rows, 8)] = jnp.zeros((8, cols), f32)
-
-        @pl.when(jnp.logical_not(bottom))
-        def _():
-            up[step].wait_recv()
-            level[pl.ds(rows, 8)] = below[step]
-
-        @pl.when(top)
-        def _():
-            flux_x[pl.ds(0, 8)] = jnp.zeros((8, cols), f32)
-
-        @pl.when(jnp.logical_not(top))
-        def _():
-            for copy in down[step]:
-                copy.wait_recv()
-            flux_x[pl.ds(0, 8)] = above_flux[step] - above_celerity[...] * (
-                level[0:1] - above_level[step]
-            )
+        flux_x[pl.ds(0, 8)] = jnp.zeros((8, cols), f32)
+        old_first = level[0:1]
 
         def strip(i, _):
             at = pl.multiple_of(i * STRIP, STRIP)
@@ -156,10 +152,7 @@
             new_level = now - (new_x - behind_x) - (new_y - behind_y)
             flux_x[pl.ds(8 + at, STRIP)] = new_x
             level[pl.ds(at, STRIP)] = new_level
-            ratio = rough[pl.ds(at, STRIP)] / jnp.maximum(new_level + bed[pl.ds(at, STRIP)], 1.0)
-            ratio = ratio.astype(bf16).astype(f32)
-            for code in range(1, 4):
-                drag[0, code - 1, pl.ds(at, STRIP), :] = with_code(ratio, code)
+            drag_of(at, new_level)
             for which, new in enumerate((new_x, new_y)):
                 for code in range(4):
                     mine = with_code(new, code)
@@ -168,7 +161,34 @@
                         settled[0, which, pl.ds(at, STRIP), :] = mine
             return 0
 
-        lax.fori_loop(0, rows // STRIP, strip, 0)
+        count = rows // STRIP
+        if step == 0:
+            lax.fori_loop(0, count // 2 - 1, strip, 0)
+            for load in loads[1]:
+                load.wait()
+            lax.fori_loop(count // 2 - 1, count - 1, strip, 0, unroll=2)
+        else:
+            lax.fori_loop(0, count - 1, strip, 0, unroll=3)
+
+        @pl.when(bottom)
+        def _():
+            level[pl.ds(rows, 8)] = jnp.zeros((8, cols), f32)
+
+        @pl.when(jnp.logical_not(bottom))
+        def _():
+            up[step].wait_recv()
+            level[pl.ds(rows, 8)] = below[step]
+
+        strip(count - 1, 0)
+
+        @pl.when(jnp.logical_not(top))
+        def _():
+            for copy in down[step]:
+                copy.wait_recv()
+            above = above_flux[step] - above_celerity[...] * (old_first - above_level[step])
+            first = lax.broadcasted_iota(jnp.int32, (8, 1), 0) == 0
+            level[pl.ds(0, 8)] = level[pl.ds(0, 8)] + jnp.where(first, pltpu.roll(above, 1, 0), 0.0)
+            drag_of(0, level[pl.ds(0, STRIP)])
 
     def settle(wanted):
         def product(pieces):
@@ -177,34 +197,32 @@
             )
             return [tall[i * side : (i + 1) * side] for i in range(len(pieces))]
 
-        def once(flip):
+        def raw(flip):
             pieces = [held[code, which] for code, which in wanted]
             mixed = [piece.astype(bf16).T for piece in product(pieces)]
-            smoothed = product(mixed)
-            out = []
-            for i, value in enumerate(smoothed):
+            return product(mixed)
+
+        def repeat(flip):
+            for i, value in enumerate(raw(flip)):
                 weight = drag[flip, wanted[i][0] - 1]
-                out.append(value * pl.reciprocal(1.0 + weight * jnp.abs(value), approx=True))
-            return out
-
-        def keep_bf16(values):
-            for i, value in enumerate(values):
-                held[wanted[i]] = value.astype(bf16)
+                value = value.astype(bf16)
+                held[wanted[i]] = value * pl.reciprocal(1 + weight * jnp.abs(value), approx=True)
 
         for code in sorted({code for code, _ in wanted}):
             drag[1, code - 1] = drag[0, code - 1].T
 
         def body(i, _):
-            keep_bf16(once(1))
-            keep_bf16(once(0))
+            repeat(1)
+            repeat(0)
             return 0
 
         lax.fori_loop(0, SUB // 2 - 1, body, 0)
-        keep_bf16(once(1))
-        values = once(0)
-        keep_bf16(values)
-        for i, value in enumerate(values):
+        repeat(1)
+        for i, value in enumerate(raw(0)):
+            weight = drag[0, wanted[i][0] - 1].astype(f32)
+            value = value / (1.0 + weight * jnp.abs(value))
             settled[wanted[i]] = value
+            held[wanted[i]] = value.astype(bf16)
 
     advance(0)
     for copy, edge in ((up[0], top), (down[0][0], bottom), (down[0][1], bottom), (down[0][2], bottom)):
@@ -221,7 +239,7 @@
         down[1][0].start()
 
     settle([(code, which) for code in (1, 2, 3) for which in range(2)])
-    flux_x[pl.ds(rows, 8)] = joined(0, rows - 8, 8)
+    rim[...] = joined(0, rows - 8, 8)
 
     @pl.when(jnp.logical_not(top))
     def _():
@@ -231,7 +249,6 @@
     def _():
         down[1][1].start()
         down[1][0].wait_send()
-        down[1][1].wait_send()
 
     advance(1)
 
@@ -243,7 +260,7 @@
         value = level[pl.ds(at, 8)]
         return sums + (1.0 + 2.0 * row / total) * (value * value)
 
-    sums = lax.fori_loop(0, rows // 8, add_up, jnp.zeros((8, cols), f32))
+    sums = lax.fori_loop(0, rows // 8, add_up, jnp.zeros((8, cols), f32), unroll=4)
     for scenario in range(2):
         share = jnp.zeros((8, 128), f32)
         for c in range(half // 128):
@@ -298,6 +315,10 @@
         keep.wait()
     for send in sends:
         send.wait()
+
+    @pl.when(jnp.logical_not(bottom))
+    def _():
+        down[1][1].wait_send()
 
 
 def write_kernel(plan, level, held, got, level_out, flux_x_out, flux_y_out, resident_out):
@@ -336,7 +357,7 @@
             pltpu.VMEM((rows, cols), f32),
             pltpu.VMEM((rows, cols), f32),
             pltpu.VMEM((rows, cols), f32),
-            pltpu.VMEM((2, 3, side, side), f32),
+            pltpu.VMEM((2, 3, side, side), bf16),
             pltpu.VMEM((side, side), bf16),
             pltpu.VMEM((4, 2, side, side), bf16),
             pltpu.VMEM((4, 2, side, side), f32),
@@ -344,10 +365,11 @@
             pltpu.VMEM((2, 8, cols), f32),
             pltpu.VMEM((2, 8, cols), f32),
             pltpu.VMEM((8, cols), f32),
+            pltpu.VMEM((8, cols), f32),
             pltpu.VMEM((n, 2, 8, 128), f32),
             pltpu.SMEM(block_plan.shape, jnp.int32),
             pltpu.VMEM((side, side), bf16),
-            pltpu.SemaphoreType.DMA((8,)),
+            pltpu.SemaphoreType.DMA((2, 8)),
             pltpu.SemaphoreType.DMA((5,)),
             pltpu.SemaphoreType.DMA((9,)),
             pltpu.SemaphoreType.DMA((9,)),
@@ -360,7 +382,7 @@
         name="window",
     )(block_plan, smoother, surface, flux_x, flux_y, celerity, bed_depth, roughness)
 
-    step = 64
+    step = 32
     flat = pl.BlockSpec((step, cols), lambda i: (i, 0))
     new_surface, new_x, new_y, resident = pl.pallas_call(
         write_kernel,

time: 46.5 us -> 44.4 us (0.955)
  Pallas kernels: 45.1 us -> 43 us
    pallas_call x1, Pallas kernels: 40.8 us -> 36.6 us  [on_device(): pl.pallas_call(functools.partial(window_kernel, n), out_shape=(jax.ShapeD...]
    pallas_call x1, Pallas kernels: 4.35 us -> 6.37 us  [on_device(): pl.pallas_call(write_kernel, grid=(rows // step,), out_shape=(jax.ShapeDt...]
where the time goes in v4:
time: 44.4 us; the launch traced here: 44.2 us
  Pallas kernels  43 us (97%)
  between operations  0.65 us (1%)
  local copies, waits for them, and re-layouts  0.52 us (1%)
    pallas_call x1, Pallas kernels, on_device(): pl.pallas_call(functools.partial(window_kernel, n), out_shape=(jax.ShapeD...  36.6 us
    pallas_call x1, Pallas kernels, on_device(): pl.pallas_call(write_kernel, grid=(rows // step,), out_shape=(jax.ShapeDt...  6.37 us

profile of v4, /device:TPU:0, one launch (start us, length us, event | category | flops | bytes accessed | tf_op | source)
XLA Modules:
  0.0 44.2 jit_solution(5705256351985602274)
XLA Ops:
  0.6 36.6 %window.1 = (f32[256,1024]{1,0:T(8,128)}, bf16[4,2,256,256]{3,2,1,0:T(8,128)(2,1)}, bf16[2,2,256,256]{3,2,1,0:T(8,128)(2,1)}, f32[2]{0:T(128)}) custom-call(s32[1,4]{1,0:T(1,128)} %plan.1, bf16[256,256]{1,0:T(8,128)(2,1)} %smoother_in.1, f32[256,1024]{1,0:T(8,128)} %surface_in.1, f32[256,1024]{1,0:T(8,128)} %flux_x_in.1, f32[256,1024]{1,0:T(8,128)} %flux_y_in.1, ...), custom_call_target="tpu_custom_call" | custom-call | tf_op jit(solution)/shard_map/window/pallas_call | solution.py:343
  37.3 0.0 copy-start
  37.3 6.4 %write_out.1 = (f32[256,1024]{1,0:T(8,128)}, f32[256,1024]{1,0:T(8,128)}, f32[256,1024]{1,0:T(8,128)}, f32[3,2,256,256]{3,2,1,0:T(8,128)}) custom-call(s32[1,4]{1,0:T(1,128)} %plan.1, f32[256,1024]{1,0:T(8,128)} %get-tuple-element.13.level, bf16[4,2,256,256]{3,2,1,0:T(8,128)(2,1)} %get-tuple-element.14.held, bf16[2,2,256,256]{3,2,1,0:T(8,128)(2,1)} %get-tuple-element.15.got), custom_call_target="tpu_custom_call" | custom-call | tf_op jit(solution)/shard_map/write_out/pallas_call | solution.py:387
  43.6 0.0 copy-done
  43.6 0.5 %copy.14 = f32[2]{0:T(128)} copy(f32[2]{0:T(128)S(1)} %copy-done) | data formatting | bytes 16
Async XLA Ops:
  37.3 6.4 %copy-start = (f32[2]{0:T(128)S(1)}, f32[2]{0:T(128)}, u32[]{:S(2)}) copy-start(f32[2]{0:T(128)} %get-tuple-element.30) | copy-start | bytes 28

commit v5 on v4

--- a/solution.py
+++ b/solution.py
@@ -18,7 +18,7 @@
     level_out, held_out, got_out, energy_out,
     level, flux_x, flux_y, celerity, bed, rough, drag, turned, held, settled,
     below, above_level, above_flux, above_celerity, rim, shares,
-    plan, s_ref, load_sem, store_sem, send_sem, recv_sem, share_send, share_recv,
+    plan, s_ref, load_sem, store_sem, keep_sem, send_sem, recv_sem, share_send, share_recv,
 ):
     rows, cols = flux_y.shape
     side = s_ref.shape[0]
@@ -154,11 +154,13 @@
             level[pl.ds(at, STRIP)] = new_level
             drag_of(at, new_level)
             for which, new in enumerate((new_x, new_y)):
-                for code in range(4):
-                    mine = with_code(new, code)
-                    held[code, which, pl.ds(at, STRIP), :] = mine.astype(bf16)
-                    if code == 0:
-                        settled[0, which, pl.ds(at, STRIP), :] = mine
+                short = new.astype(bf16)
+                for code in range(1, 4):
+                    held[code, which, pl.ds(at, STRIP), :] = with_code(short, code)
+                if step < STEPS - 1:
+                    settled[0, which, pl.ds(at, STRIP), :] = with_code(new, 0)
+                else:
+                    held[0, which, pl.ds(at, STRIP), :] = with_code(short, 0)
             return 0
 
         count = rows // STRIP
@@ -190,7 +192,7 @@
             level[pl.ds(0, 8)] = level[pl.ds(0, 8)] + jnp.where(first, pltpu.roll(above, 1, 0), 0.0)
             drag_of(0, level[pl.ds(0, STRIP)])
 
-    def settle(wanted):
+    def settle(wanted, step):
         def product(pieces):
             tall = jnp.dot(
                 jnp.concatenate(pieces, 0), turned[...], preferred_element_type=f32
@@ -221,7 +223,8 @@
         for i, value in enumerate(raw(0)):
             weight = drag[0, wanted[i][0] - 1].astype(f32)
             value = value / (1.0 + weight * jnp.abs(value))
-            settled[wanted[i]] = value
+            if step < STEPS - 1:
+                settled[wanted[i]] = value
             held[wanted[i]] = value.astype(bf16)
 
     advance(0)
@@ -238,7 +241,7 @@
     def _():
         down[1][0].start()
 
-    settle([(code, which) for code in (1, 2, 3) for which in range(2)])
+    settle([(code, which) for code in (1, 2, 3) for which in range(2)], 0)
     rim[...] = joined(0, rows - 8, 8)
 
     @pl.when(jnp.logical_not(top))
@@ -286,18 +289,21 @@
 
     sends = []
     keeps = [keep_dry]
-    for code in (3, 2):
-        settle([(code, 0), (code, 1), (1, 3 - code)])
-        hop = code - 1
-        send = remote(held.at[code], got_out.at[hop - 1], 6 + hop, lax.rem(me + hop, n))
-        send.start()
-        sends.append(send)
-        keep = pltpu.make_async_copy(held.at[code], held_out.at[code], store_sem.at[code])
-        keep.start()
-        keeps.append(keep)
-    keep = pltpu.make_async_copy(held.at[1], held_out.at[1], store_sem.at[1])
-    keep.start()
-    keeps.append(keep)
+    for group in (((3, 0), (3, 1), (2, 0)), ((2, 1), (1, 0), (1, 1))):
+        settle(group, 1)
+        for code, which in group:
+            if code > 1:
+                hop = code - 1
+                send = remote(
+                    held.at[code, which], got_out.at[hop - 1, which], 5 + 2 * hop + which, lax.rem(me + hop, n)
+                )
+                send.start()
+                sends.append(send)
+            keep = pltpu.make_async_copy(
+                held.at[code, which], held_out.at[code, which], keep_sem.at[2 * code - 2 + which]
+            )
+            keep.start()
+            keeps.append(keep)
 
     def gather(d, _):
         share_copy(d).wait()
@@ -371,8 +377,9 @@
             pltpu.VMEM((side, side), bf16),
             pltpu.SemaphoreType.DMA((2, 8)),
             pltpu.SemaphoreType.DMA((5,)),
-            pltpu.SemaphoreType.DMA((9,)),
-            pltpu.SemaphoreType.DMA((9,)),
+            pltpu.SemaphoreType.DMA((6,)),
+            pltpu.SemaphoreType.DMA((11,)),
+            pltpu.SemaphoreType.DMA((11,)),
             pltpu.SemaphoreType.DMA((n - 1,)),
             pltpu.SemaphoreType.DMA((n - 1,)),
         ],
@@ -382,7 +389,7 @@
         name="window",
     )(block_plan, smoother, surface, flux_x, flux_y, celerity, bed_depth, roughness)
 
-    step = 32
+    step = 128
     flat = pl.BlockSpec((step, cols), lambda i: (i, 0))
     new_surface, new_x, new_y, resident = pl.pallas_call(
         write_kernel,

time: 44.4 us -> 41.4 us (0.932)
  Pallas kernels: 43 us -> 40.1 us
    pallas_call x1, Pallas kernels: 6.37 us -> 3.56 us  [on_device(): pl.pallas_call(write_kernel, grid=(rows // step,), out_shape=(jax.ShapeDt...]
where the time goes in v5:
time: 41.4 us; the launch traced here: 41.3 us
  Pallas kernels  40.1 us (97%)
  between operations  0.65 us (2%)
  local copies, waits for them, and re-layouts  0.52 us (1%)
    pallas_call x1, Pallas kernels, on_device(): pl.pallas_call(functools.partial(window_kernel, n), out_shape=(jax.ShapeD...  36.5 us
    pallas_call x1, Pallas kernels, on_device(): pl.pallas_call(write_kernel, grid=(rows // step,), out_shape=(jax.ShapeDt...  3.56 us

profile of v5, /device:TPU:0, one launch (start us, length us, event | category | flops | bytes accessed | tf_op | source)
XLA Modules:
  0.0 41.3 jit_solution(18359722631156113930)
XLA Ops:
  0.6 36.5 %window.1 = (f32[256,1024]{1,0:T(8,128)}, bf16[4,2,256,256]{3,2,1,0:T(8,128)(2,1)}, bf16[2,2,256,256]{3,2,1,0:T(8,128)(2,1)}, f32[2]{0:T(128)}) custom-call(s32[1,4]{1,0:T(1,128)} %plan.1, bf16[256,256]{1,0:T(8,128)(2,1)} %smoother_in.1, f32[256,1024]{1,0:T(8,128)} %surface_in.1, f32[256,1024]{1,0:T(8,128)} %flux_x_in.1, f32[256,1024]{1,0:T(8,128)} %flux_y_in.1, ...), custom_call_target="tpu_custom_call" | custom-call | tf_op jit(solution)/shard_map/window/pallas_call | solution.py:349
  37.2 0.0 copy-start
  37.2 3.6 %write_out.1 = (f32[256,1024]{1,0:T(8,128)}, f32[256,1024]{1,0:T(8,128)}, f32[256,1024]{1,0:T(8,128)}, f32[3,2,256,256]{3,2,1,0:T(8,128)}) custom-call(s32[1,4]{1,0:T(1,128)} %plan.1, f32[256,1024]{1,0:T(8,128)} %get-tuple-element.13.level, bf16[4,2,256,256]{3,2,1,0:T(8,128)(2,1)} %get-tuple-element.14.held, bf16[2,2,256,256]{3,2,1,0:T(8,128)(2,1)} %get-tuple-element.15.got), custom_call_target="tpu_custom_call" | custom-call | tf_op jit(solution)/shard_map/write_out/pallas_call | solution.py:394
  40.7 0.0 copy-done
  40.7 0.5 %copy.14 = f32[2]{0:T(128)} copy(f32[2]{0:T(128)S(1)} %copy-done) | data formatting | bytes 16
Async XLA Ops:
  37.2 3.6 %copy-start = (f32[2]{0:T(128)S(1)}, f32[2]{0:T(128)}, u32[]{:S(2)}) copy-start(f32[2]{0:T(128)} %get-tuple-element.30) | copy-start | bytes 28

commit v6 on v5

--- a/solution.py
+++ b/solution.py
@@ -389,7 +389,7 @@
         name="window",
     )(block_plan, smoother, surface, flux_x, flux_y, celerity, bed_depth, roughness)
 
-    step = 128
+    step = rows
     flat = pl.BlockSpec((step, cols), lambda i: (i, 0))
     new_surface, new_x, new_y, resident = pl.pallas_call(
         write_kernel,

time: 41.4 us -> 41.8 us (level)
  no operation moved by 1% of the time
where the time goes in v6:
time: 41.8 us; the launch traced here: 41.7 us
  Pallas kernels  40.5 us (97%)
  between operations  0.65 us (2%)
  local copies, waits for them, and re-layouts  0.52 us (1%)
    pallas_call x1, Pallas kernels, on_device(): pl.pallas_call(functools.partial(window_kernel, n), out_shape=(jax.ShapeD...  36.5 us
    pallas_call x1, Pallas kernels, on_device(): pl.pallas_call(write_kernel, grid=(rows // step,), out_shape=(jax.ShapeDt...  3.96 us

profile of v6, /device:TPU:0, one launch (start us, length us, event | category | flops | bytes accessed | tf_op | source)
XLA Modules:
  0.0 41.7 jit_solution(6191931617741650075)
XLA Ops:
  0.6 36.5 %window.1 = (f32[256,1024]{1,0:T(8,128)}, bf16[4,2,256,256]{3,2,1,0:T(8,128)(2,1)}, bf16[2,2,256,256]{3,2,1,0:T(8,128)(2,1)}, f32[2]{0:T(128)}) custom-call(s32[1,4]{1,0:T(1,128)} %plan.1, bf16[256,256]{1,0:T(8,128)(2,1)} %smoother_in.1, f32[256,1024]{1,0:T(8,128)} %surface_in.1, f32[256,1024]{1,0:T(8,128)} %flux_x_in.1, f32[256,1024]{1,0:T(8,128)} %flux_y_in.1, ...), custom_call_target="tpu_custom_call" | custom-call | tf_op jit(solution)/shard_map/window/pallas_call | solution.py:349
  37.2 0.0 copy-start
  37.2 4.0 %write_out.1 = (f32[256,1024]{1,0:T(8,128)}, f32[256,1024]{1,0:T(8,128)}, f32[256,1024]{1,0:T(8,128)}, f32[3,2,256,256]{3,2,1,0:T(8,128)}) custom-call(s32[1,4]{1,0:T(1,128)} %plan.1, f32[256,1024]{1,0:T(8,128)} %get-tuple-element.13.level, bf16[4,2,256,256]{3,2,1,0:T(8,128)(2,1)} %get-tuple-element.14.held, bf16[2,2,256,256]{3,2,1,0:T(8,128)(2,1)} %get-tuple-element.15.got), custom_call_target="tpu_custom_call" | custom-call | tf_op jit(solution)/shard_map/write_out/pallas_call | solution.py:394
  41.1 0.0 copy-done
  41.1 0.5 %copy.14 = f32[2]{0:T(128)} copy(f32[2]{0:T(128)S(1)} %copy-done) | data formatting | bytes 16
Async XLA Ops:
  37.2 4.0 %copy-start = (f32[2]{0:T(128)S(1)}, f32[2]{0:T(128)}, u32[]{:S(2)}) copy-start(f32[2]{0:T(128)} %get-tuple-element.30) | copy-start | bytes 28
